TPU v7x, 128 devices: a whole 4x4x4 slice. The times are simulated.
128 devices in a mesh: queue: 16 (over z_hi, x, core), tile: 8 (over y, z_lo).
Axes of the slice: x: 4, y: 4, z: 4 (z_hi: 2, z_lo: 2; z = z_hi * 2 + z_lo), core: 2. Of those that a mesh axis runs over, the one named last changes fastest.
Arguments:
- queue_latents: float32 [128, 4, 16, 128], P('queue', None, 'tile'), may hold values from -6 to 6
- entering: float32 [2, 4, 16, 128], P(None, None, 'tile'), may hold values from -6 to 6
- levels: int32 [128], P('queue'), may hold values from 1 to 896, as said below
- time_weight: float32 [320, 320], replicated, may hold values from -0.3125 to 0.3125
- conv_in_weight: bfloat16 [3, 3, 4, 320], replicated, may hold values from -1 to 1
- conv_mid_weight: bfloat16 [3, 3, 320, 320], replicated, may hold values from -0.109375 to 0.109375
- norm_gain: float32 [320], replicated, may hold values from 0.1 to 1.9
- qkv_weight: bfloat16 [320, 960], replicated, may hold values from -0.3125 to 0.3125
- head_scale: float32 [5], replicated, may hold values from 2 to 12
- attn_out_weight: bfloat16 [320, 320], replicated, may hold values from -0.3125 to 0.3125
- eps_out_weight: bfloat16 [320, 4], replicated, may hold values from -0.3125 to 0.3125
Outputs:
- final_queue: float32 [128, 4, 16, 128], P('queue', None, 'tile')
Inputs may be any that keep to these rules, and one draw needn't show every extreme that they name: `levels`: strictly rising over the slots; the last slot's level is exactly the maximum.
All inputs are finite; a program needn't handle non-finite values.
Results may differ from a plain program's by a relative error of at most 0.0012.
Values may be sent and summed in bfloat16 or wider, within the bound.
A program may use at most 128 MiB of HBM per device.

v0:
```python
import math

import jax
import jax.numpy as jnp
from jax import lax
from jax.experimental import pallas as pl
from jax.experimental.pallas import tpu as pltpu
from jax.sharding import PartitionSpec as P

WIN = 8
STEPS = 2
F32 = jnp.float32
BF16 = jnp.bfloat16
MESH = pl.DeviceIdType.MESH

CH = 320
HEADS = 5
HD = 64
FR = 128
NQ = 16
NT = 8
PX = 8
ROW = 48
TAPS = 3 * ROW


def dot(a, b):
    return jnp.dot(a, b, preferred_element_type=F32)


def dot_t(a, b):
    return lax.dot_general(a, b, (((0,), (0,)), ((), ())), preferred_element_type=F32)


def sin_cos(angle):
    count = jnp.floor(angle * (2.0 / math.pi) + 0.5)
    rest = ((angle - count * 1.5703125) - count * 4.837512969970703125e-4) - count * 7.54978995489188216e-8
    square = rest * rest
    sine = rest + rest * square * (
        -1.6666654611e-1 + square * (8.3321608736e-3 - square * 1.9515295891e-4)
    )
    cosine = 1.0 - 0.5 * square + square * square * (
        4.166664568298827e-2 + square * (-1.388731625493765e-3 + square * 2.443315711809948e-5)
    )
    quarter = count - 4.0 * jnp.floor(count * 0.25)
    odd = (quarter == 1.0) | (quarter == 3.0)
    sin_out = jnp.where(odd, cosine, sine)
    cos_out = jnp.where(odd, sine, cosine)
    sin_out = jnp.where(quarter >= 2.0, -sin_out, sin_out)
    cos_out = jnp.where((quarter == 1.0) | (quarter == 2.0), -cos_out, cos_out)
    return sin_out, cos_out


def silu(x):
    half = 0.5 * x
    return half + half * jnp.tanh(half)


def lanes(shape):
    return lax.broadcasted_iota(jnp.int32, shape, 1)


def pack_latents(lat_ref, lev_ref, send_ref):
    lane = lanes((8, FR))
    row = lax.broadcasted_iota(jnp.int32, (8, FR), 0)
    pieces = []
    for c in range(4):
        for r in range(2):
            plane = lat_ref[:, c, r, :]
            own, left, right = c * 16 + r * 8, 64 + r * 8 + c * 2, 80 + r * 8 + c * 2
            pieces.append((3, own, pltpu.roll(plane, own, 1)))
            pieces.append((1, left, pltpu.roll(plane, left + 2, 1)))
            pieces.append((1, right, pltpu.roll(plane, right - 8, 1)))
    level = jnp.zeros((8, FR), F32)
    for f in range(8):
        level = jnp.where(row == f, lev_ref[f].astype(F32), level)

    def body(dest, carry):
        place = (lane - 8 * dest) & (FR - 1)
        total = jnp.zeros((8, FR), F32)
        for bits, base, plane in pieces:
            total = jnp.where((place >> bits) == (base >> bits), plane, total)
        total = pltpu.roll(total, lax.rem(FR - 8 * dest, FR), 1)
        send_ref[dest] = jnp.where(lane == 2 * ROW, level, total)
        return carry

    lax.fori_loop(0, NQ, body, 0)


def prepare(cin_ref, cmid_ref, gain_ref, qkv_ref, wo_ref, we_ref, ent_ref, taps_ref,
            band_ref, mid_ref, qkvt_ref, wot_ref, wet_ref, gain_out, near_ref, ent_out, q):
    taps_ref[...] = jnp.zeros(taps_ref.shape, F32)
    for i in range(9):
        taps_ref[4 * i : 4 * i + 4, :] = cin_ref[i // 3, i % 3].astype(F32)
    taps_t = taps_ref[...].T.astype(BF16)
    k = lanes((40, TAPS))
    m = lax.broadcasted_iota(jnp.int32, (40, TAPS), 0)
    dy = (k >= ROW).astype(jnp.int32) + (k >= 2 * ROW).astype(jnp.int32)
    rest = k - ROW * dy
    own = rest < 32
    left = rest < 40
    c = jnp.where(own, rest >> 3, (rest & 7) >> 1)
    rel = jnp.where(own, (rest & 7) + 2, jnp.where(left, rest & 1, (rest & 1) + 10))
    for w in range(PX + 2):
        dx = rel - w
        pick = (dx >= 0) & (dx <= 2) & (m == dy * 12 + dx * 4 + c)
        band_ref[w] = dot(taps_t, jnp.where(pick, 1.0, 0.0).astype(BF16)).astype(BF16)
    for dx in range(3):
        for dy_ in range(3):
            mid_ref[dx, dy_] = cmid_ref[dy_, dx].T
    qkvt_ref[...] = qkv_ref[...].T
    wot_ref[...] = wo_ref[...].T
    eps = jnp.concatenate([we_ref[...].astype(F32), jnp.zeros((CH, FR - 4), F32)], axis=1)
    wet_ref[...] = eps.T[:16].astype(BF16)
    gain_out[...] = jnp.broadcast_to(gain_ref[...], (FR, CH)).T
    key_slot = lax.broadcasted_iota(jnp.int32, (FR, FR), 0)
    query_slot = lanes((FR, FR))
    near_ref[...] = jnp.where(jnp.abs(key_slot - query_slot) <= WIN, 1.0, 0.0).astype(BF16)
    lane = lanes((8, FR))
    for s in range(STEPS):
        rows = jnp.concatenate([ent_ref[s, c, r : r + 1, :] for c in range(4) for r in range(2)], axis=0)
        rows = pltpu.roll(rows, lax.rem(FR - 8 * q, FR), 1)
        columns = jnp.concatenate([rows, jnp.zeros((FR - 8, FR), F32)], axis=0).T[:8]
        for i in range(8):
            shifted = pltpu.roll(columns, FR - 1 - i, 1)
            ent_out[s, 8 * i : 8 * i + 8, :] = jnp.where(lane == FR - 1, shifted, 0.0)


def embed(level, tw_ref, emb_ref):
    index = lax.broadcasted_iota(jnp.int32, (CH // 2, FR), 0).astype(F32)
    freqs = jnp.exp(-math.log(10000.0) * index / (CH // 2))
    sine, cosine = sin_cos(level * freqs)
    feature = jnp.concatenate([sine, cosine], axis=0)
    emb_ref[...] = lax.dot_general(
        tw_ref[...].T, feature, (((1,), (0,)), ((), ())),
        precision=lax.Precision.HIGHEST, preferred_element_type=F32)


def coefficients(level):
    lane = lanes((8, FR))
    level = jnp.broadcast_to(level, (8, FR))
    target = jnp.where(lane == 0, 0.0, pltpu.roll(level, 1, 1))
    angle = lambda l: (l / 1000.0 + 0.008) / 1.008 * (math.pi / 2.0)
    s0, c0 = sin_cos(angle(level))
    s1, c1 = sin_cos(angle(target))
    alpha = c1 / c0
    return alpha, s1 - alpha * s0


def conv_in(slots, band_ref, emb_ref, rhs_ref, hid_ref, act_ref, q, t):
    rows = []
    for slot in slots:
        for r in range(2):
            rows.append(jnp.concatenate(
                [slot[g * 16 + r * 8 : g * 16 + r * 8 + 8] for g in range(6)], axis=0).astype(BF16))
    for p in range(2):
        for half in range(2):
            rhs_ref[p, :, half * FR : (half + 1) * FR] = jnp.concatenate(
                rows[2 * p + half : 2 * p + half + 3], axis=0)

    def body(w, carry):
        for p in range(2):
            both = dot(band_ref[w], rhs_ref[p])
            for half in range(2):
                hidden = both[:, half * FR : (half + 1) * FR] + emb_ref[...]
                act_ref[w, 2 * p + half] = silu(hidden).astype(BF16)
                if p != half:
                    hid_ref[w, p] = hidden
        return carry

    lax.fori_loop(0, PX + 2, body, 0)

    @pl.when(t == 0)
    def _():
        for w in range(PX + 2):
            act_ref[w, 0] = jnp.zeros((CH, FR), BF16)

    @pl.when(t == NT - 1)
    def _():
        for w in range(PX + 2):
            act_ref[w, 3] = jnp.zeros((CH, FR), BF16)

    @pl.when(q == 0)
    def _():
        for r in range(4):
            act_ref[0, r] = jnp.zeros((CH, FR), BF16)

    @pl.when(q == NQ - 1)
    def _():
        for r in range(4):
            act_ref[PX + 1, r] = jnp.zeros((CH, FR), BF16)


def unit(x, scale):
    return (x * (lax.rsqrt(jnp.sum(x * x, axis=0, keepdims=True) + 1e-06) * scale)).astype(BF16)


def block_net(hs_ref, mid_ref, qkvt_ref, wot_ref, wet_ref, gain_ref, near_ref, hid_ref, act_ref, noise_ref):
    def body(i, carry):
        r, j = lax.div(i, 4), lax.rem(i, 4)
        block = jnp.concatenate([hid_ref[2 * j + 1, r], hid_ref[2 * j + 2, r]], axis=1)
        for dx in range(3):
            rhs = jnp.concatenate(
                [act_ref[2 * j + dx + s, pl.ds(r, 3)].reshape(3 * CH, FR) for s in range(2)], axis=1)
            lhs = jnp.concatenate([mid_ref[dx, dy] for dy in range(3)], axis=1)
            block = block + dot(lhs, rhs)
        center = jnp.mean(block, axis=0, keepdims=True)
        moved = block - center
        spread = jnp.mean(moved * moved, axis=0, keepdims=True)
        gain = jnp.concatenate([gain_ref[...]] * 2, axis=1)
        normed = (moved * lax.rsqrt(spread + 1e-05) * gain).astype(BF16)
        project = dot(qkvt_ref[...], normed)
        mixed = []
        for h in range(HEADS):
            query = unit(project[h * HD : (h + 1) * HD], hs_ref[h] * math.log2(math.e))
            key = unit(project[CH + h * HD : CH + (h + 1) * HD], 1.0)
            value = project[2 * CH + h * HD : 2 * CH + (h + 1) * HD].astype(BF16)
            value = jnp.concatenate([value, jnp.ones((16, 2 * FR), BF16)], axis=0)
            parts = []
            for s in range(2):
                cut = slice(s * FR, (s + 1) * FR)
                scores = dot_t(key[:, cut], query[:, cut])
                weights = jnp.exp2(scores).astype(BF16) * near_ref[...]
                total = dot(value[:, cut], weights)
                parts.append((total[:HD] / total[HD : HD + 1]).astype(BF16))
            mixed.append(jnp.concatenate(parts, axis=1))
        upper = block + dot(wot_ref[...], jnp.concatenate(mixed, axis=0))
        noise_ref[i] = dot(wet_ref[...], silu(upper).astype(BF16))[:8]
        return carry

    lax.fori_loop(0, PX, body, 0)


def advance(state, noise_ref, alpha, beta, entering):
    tiles = []
    for c in range(4):
        for r in range(2):
            rows = [noise_ref[r * 4 + w // 2, c : c + 1, (w % 2) * FR : (w % 2 + 1) * FR] for w in range(PX)]
            noise = jnp.concatenate(rows, axis=0)
            at = c * 16 + r * 8
            tiles.append(alpha * state[at : at + 8] + beta * noise)
    updated = jnp.concatenate(tiles, axis=0)
    return jnp.where(lanes((64, FR)) == FR - 1, entering, pltpu.roll(updated, FR - 1, 1))


def masked(slot, index, q, t):
    inside = (t > 0) if index == 0 else (t < NT - 1) if index == 2 else None
    own, left, right = slot[:64], slot[64:80], slot[80:96]
    left = jnp.where(q > 0, left, 0.0)
    right = jnp.where(q < NQ - 1, right, 0.0)
    slot = jnp.concatenate([own, left, right], axis=0)
    return slot if inside is None else jnp.where(inside, slot, 0.0)


def kernel(lat_ref, ent_ref, lev_ref, tw_hbm, cin_ref, cmid_hbm, gain_ref, qkv_hbm, hs_ref, wo_hbm, we_ref,
           out_ref,
           tw_ref, cmid_ref, qkv_ref, wo_ref, taps_ref,
           band_ref, mid_ref, qkvt_ref, wot_ref, wet_ref, gain_out, near_ref, ent_out,
           emb_ref, rhs_ref, hid_ref, act_ref, noise_ref,
           send1, recv1, halo, own_ref, left_ref, right_ref, send3, recv3,
           load_sem, send1_sem, recv1_sem, send2_sem, recv2_sem, send3_sem, recv3_sem):
    q, t = lax.axis_index("queue"), lax.axis_index("tile")
    loads = [pltpu.make_async_copy(src, dst, load_sem.at[i]) for i, (src, dst) in enumerate(
        [(cmid_hbm, cmid_ref), (qkv_hbm, qkv_ref), (wo_hbm, wo_ref), (tw_hbm, tw_ref)])]
    for load in loads:
        load.start()

    barrier = pltpu.get_barrier_semaphore()
    above, below = lax.rem(t + NT - 1, NT), lax.rem(t + 1, NT)

    def greet(k, carry):
        peer = lax.rem(q + k, NQ)
        pl.semaphore_signal(barrier, inc=1, device_id=(peer, above), device_id_type=MESH)
        pl.semaphore_signal(barrier, inc=1, device_id=(peer, below), device_id_type=MESH)
        return carry

    def greet_row(k, carry):
        pl.semaphore_signal(barrier, inc=1, device_id=(lax.rem(q + k, NQ), t), device_id_type=MESH)
        return carry

    lax.fori_loop(0, NQ, greet, 0)
    lax.fori_loop(1, NQ, greet_row, 0)
    pack_latents(lat_ref, lev_ref, send1)
    pl.semaphore_wait(barrier, 3 * NQ - 1)

    place = pl.ds(pl.multiple_of(q * 8, 8), 8)

    def to_peer(peer, row, slot):
        pltpu.make_async_remote_copy(
            src_ref=send1.at[peer], dst_ref=recv1.at[slot, place],
            send_sem=send1_sem.at[slot], recv_sem=recv1_sem.at[slot],
            device_id=(peer, row), device_id_type=MESH).start()

    def scatter_row(k, carry):
        to_peer(lax.rem(q + k, NQ), t, 1)
        return carry

    def scatter(k, carry):
        peer = lax.rem(q + k, NQ)
        to_peer(peer, above, 2)
        to_peer(peer, below, 0)
        return carry

    lax.fori_loop(1, NQ, scatter_row, 0)
    lax.fori_loop(0, NQ, scatter, 0)
    recv1[1, place] = send1[q]

    for load in loads:
        load.wait()
    prepare(cin_ref, cmid_ref, gain_ref, qkv_ref, wo_ref, we_ref, ent_ref, taps_ref,
            band_ref, mid_ref, qkvt_ref, wot_ref, wet_ref, gain_out, near_ref, ent_out, q)

    for slot in range(3):
        count = FR if slot != 1 else FR - 8
        part = recv1.at[slot, pl.ds(0, count)]
        pltpu.make_async_copy(part, part, recv1_sem.at[slot]).wait()
    slots = [recv1[slot].T for slot in range(3)]
    level = slots[1][2 * ROW : 2 * ROW + 1]
    embed(level, tw_ref, emb_ref)
    alpha, beta = coefficients(level)
    state = slots[1][:64]
    slots = [masked(slot[: 2 * ROW], i, q, t) for i, slot in enumerate(slots)]

    conv_in(slots, band_ref, emb_ref, rhs_ref, hid_ref, act_ref, q, t)
    block_net(hs_ref, mid_ref, qkvt_ref, wot_ref, wet_ref, gain_out, near_ref, hid_ref, act_ref, noise_ref)
    state = advance(state, noise_ref, alpha, beta, ent_out[0])

    own_ref[...] = state
    for r in range(2):
        for c in range(4):
            at = c * 16 + r * 8
            left_ref[r * 8 + c * 2 : r * 8 + c * 2 + 2, :] = state[at + 6 : at + 8]
            right_ref[r * 8 + c * 2 : r * 8 + c * 2 + 2, :] = state[at : at + 2]
    before, after = lax.rem(q + NQ - 1, NQ), lax.rem(q + 1, NQ)
    copies = []
    for row, slot in ((t, 1), (above, 2), (below, 0)):
        if slot != 1:
            copies.append((own_ref, (0, 64), q, row, slot))
        copies.append((left_ref, (64, 16), after, row, slot))
        copies.append((right_ref, (80, 16), before, row, slot))
    copies = [
        pltpu.make_async_remote_copy(
            src_ref=src, dst_ref=halo.at[slot, pl.ds(start, size)],
            send_sem=send2_sem.at[i], recv_sem=recv2_sem.at[i],
            device_id=(peer, row), device_id_type=MESH)
        for i, (src, (start, size), peer, row, slot) in enumerate(copies)]
    for copy in copies:
        copy.start()
    for copy in copies:
        copy.wait_recv()
    halo[1, :64] = own_ref[...]
    slots = [masked(halo[i], i, q, t) for i in range(3)]

    conv_in(slots, band_ref, emb_ref, rhs_ref, hid_ref, act_ref, q, t)
    block_net(hs_ref, mid_ref, qkvt_ref, wot_ref, wet_ref, gain_out, near_ref, hid_ref, act_ref, noise_ref)
    state = advance(own_ref[...], noise_ref, alpha, beta, ent_out[1])

    frames = jnp.concatenate([state, jnp.zeros((64, FR), F32)], axis=0).T
    for peer in range(NQ):
        send3[peer] = frames[peer * 8 : peer * 8 + 8]

    def give(k, carry):
        peer = lax.rem(q + k, NQ)
        pltpu.make_async_remote_copy(
            src_ref=send3.at[peer], dst_ref=recv3.at[q],
            send_sem=send3_sem.at[0], recv_sem=recv3_sem.at[0],
            device_id=(peer, t), device_id_type=MESH).start()
        return carry

    lax.fori_loop(1, NQ, give, 0)
    recv3[q] = send3[q]
    for copy in copies:
        copy.wait_send()
    for slot in range(3):
        part = send1.at[pl.ds(0, NQ if slot != 1 else NQ - 1)]
        pltpu.make_async_copy(part, part, send1_sem.at[slot]).wait()
    part = recv3.at[pl.ds(0, NQ - 1)]
    pltpu.make_async_copy(part, part, recv3_sem.at[0]).wait()
    part = send3.at[pl.ds(0, NQ - 1)]
    pltpu.make_async_copy(part, part, send3_sem.at[0]).wait()

    lane = lanes((8, FR))
    for c in range(4):
        for r in range(2):
            at = c * 16 + r * 8
            total = jnp.zeros((8, FR), F32)
            for source in range(NQ):
                moved = pltpu.roll(recv3[source], (FR + 8 * source - at) % FR, 1)
                total = jnp.where((lane >> 3) == source, moved, total)
            out_ref[:, c, r, :] = total


def per_device(queue_latents, entering, levels, time_weight, conv_in_weight, conv_mid_weight, norm_gain,
               qkv_weight, head_scale, attn_out_weight, eps_out_weight):
    vmem = pl.BlockSpec(memory_space=pltpu.VMEM)
    smem = pl.BlockSpec(memory_space=pltpu.SMEM)
    hbm = pl.BlockSpec(memory_space=pl.ANY)
    v = pltpu.VMEM
    dma = pltpu.SemaphoreType.DMA
    return pl.pallas_call(
        kernel,
        out_shape=jax.ShapeDtypeStruct(queue_latents.shape, F32),
        in_specs=[vmem, vmem, smem, hbm, vmem, hbm, vmem, hbm, smem, hbm, vmem],
        out_specs=vmem,
        scratch_shapes=[
            v((CH, CH), F32), v((3, 3, CH, CH), BF16), v((CH, 3 * CH), BF16), v((CH, CH), BF16), v((40, CH), F32),
            v((PX + 2, CH, TAPS), BF16), v((3, 3, CH, CH), BF16), v((3 * CH, CH), BF16), v((CH, CH), BF16),
            v((16, CH), BF16), v((CH, FR), F32), v((FR, FR), BF16), v((STEPS, 64, FR), F32),
            v((CH, FR), F32), v((2, TAPS, 2 * FR), BF16), v((PX + 2, 2, CH, FR), F32),
            v((PX + 2, 4, CH, FR), BF16), v((PX, 8, 2 * FR), F32),
            v((NQ, 8, FR), F32), v((3, FR, FR), F32), v((3, 2 * ROW, FR), F32), v((64, FR), F32),
            v((16, FR), F32), v((16, FR), F32), v((NQ, 8, FR), F32), v((NQ, 8, FR), F32),
            dma((4,)), dma((3,)), dma((3,)), dma((8,)), dma((8,)), dma((1,)), dma((1,)),
        ],
        compiler_params=pltpu.CompilerParams(
            collective_id=0, has_side_effects=True, vmem_limit_bytes=56 * 1024 * 1024),
    )(queue_latents, entering, levels, time_weight, conv_in_weight, conv_mid_weight,
      norm_gain.reshape(1, CH), qkv_weight, head_scale, attn_out_weight, eps_out_weight)


def solution(mesh):
    placed = (
        P("queue", None, "tile", None),
        P(None, None, "tile", None),
        P("queue"),
        P(),
        P(),
        P(),
        P(),
        P(),
        P(),
        P(),
        P(),
    )
    return jax.shard_map(
        per_device,
        mesh=mesh,
        in_specs=placed,
        out_specs=P("queue", None, "tile", None),
        check_vma=False,
    )
```

profile of v0, /device:TPU:1, one launch (start us, length us, event | category | flops | bytes accessed | tf_op | source)
XLA Modules:
  0.0 101.1 jit_solution(2278003112336326846)
XLA Ops:
  0.0 1.2 %reshape.3.gain_ref = f32[1,320]{1,0:T(1,128)} reshape(f32[320]{0:T(512)} %param.17) | data formatting | bytes 2560 | tf_op jit(solution)/shard_map/reshape | solution.py:418
  1.2 1.4 %copy.12.we_ref = bf16[320,4]{1,0:T(8,128)(2,1)} copy(bf16[320,4]{0,1:T(4,128)(2,1)} %param.21) | data formatting | bytes 5120 | tf_op args[10]
  2.7 97.1 %shard_map.109 = f32[8,4,2,128]{3,2,1,0:T(2,128)} custom-call(f32[8,4,2,128]{3,2,1,0:T(2,128)} %lat_ref.1, f32[2,4,2,128]{3,2,1,0:T(2,128)} %ent_ref.1, s32[8]{0:T(128)} %lev_ref.1, f32[320,320]{1,0:T(8,128)} %tw_hbm.1, bf16[3,3,4,320]{3,2,1,0:T(4,128)(2,1)} %cin_ref.1, bf16[3,3,320,320]{3,2,1,0:T(8,128)(2,1)} %cmid_hbm.1, f32[1,320]{1,0:T(1,128)} %reshape.3.gain_ref, ...), custom_call_target="tpu_custom_call" | custom-call | tf_op jit(solution)/shard_map/pallas_call | solution.py:400
  99.8 1.4 %copy.14 = f32[8,4,2,128]{3,2,1,0:T(2,128)} copy(f32[8,4,2,128]{3,2,1,0:T(2,128)} %shard_map.109) | data formatting | bytes 65536
where the time goes:
time: 101 us
  Pallas kernels  97.1 us (96%)
  local copies, waits for them, and re-layouts  4.06 us (4%)
    pallas_call x1, Pallas kernels, per_device(): pl.pallas_call(kernel, out_shape=jax.ShapeDtypeStruct(queue_latents.shape...  97.1 us
    unnamed x2, local copies, waits for them, and re-layouts  2.82 us

commit v1 on v0

--- a/solution.py
+++ b/solution.py
@@ -106,8 +106,7 @@
         pick = (dx >= 0) & (dx <= 2) & (m == dy * 12 + dx * 4 + c)
         band_ref[w] = dot(taps_t, jnp.where(pick, 1.0, 0.0).astype(BF16)).astype(BF16)
     for dx in range(3):
-        for dy_ in range(3):
-            mid_ref[dx, dy_] = cmid_ref[dy_, dx].T
+        mid_ref[dx] = jnp.concatenate([cmid_ref[dy_, dx] for dy_ in range(3)], axis=0).T
     qkvt_ref[...] = qkv_ref[...].T
     wot_ref[...] = wo_ref[...].T
     eps = jnp.concatenate([we_ref[...].astype(F32), jnp.zeros((CH, FR - 4), F32)], axis=1)
@@ -168,7 +167,7 @@
                     hid_ref[w, p] = hidden
         return carry
 
-    lax.fori_loop(0, PX + 2, body, 0)
+    lax.fori_loop(0, PX + 2, body, 0, unroll=5)
 
     @pl.when(t == 0)
     def _():
@@ -195,40 +194,77 @@
     return (x * (lax.rsqrt(jnp.sum(x * x, axis=0, keepdims=True) + 1e-06) * scale)).astype(BF16)
 
 
-def block_net(hs_ref, mid_ref, qkvt_ref, wot_ref, wet_ref, gain_ref, near_ref, hid_ref, act_ref, noise_ref):
-    def body(i, carry):
+def each_pair(bodies):
+    def step(i, carry):
+        for body in bodies:
+            body(i)
+        return carry
+
+    lax.fori_loop(0, PX, step, 0, unroll=PX)
+
+
+def block_net(hs_ref, mid_ref, qkvt_ref, wot_ref, wet_ref, gain_ref, near_ref, hid_ref, act_ref, noise_ref,
+              block_ref, normed_ref, project_ref, unit_ref, key_ref, weight_ref, mixed_ref):
+    def conv_mid(i):
         r, j = lax.div(i, 4), lax.rem(i, 4)
         block = jnp.concatenate([hid_ref[2 * j + 1, r], hid_ref[2 * j + 2, r]], axis=1)
         for dx in range(3):
             rhs = jnp.concatenate(
                 [act_ref[2 * j + dx + s, pl.ds(r, 3)].reshape(3 * CH, FR) for s in range(2)], axis=1)
-            lhs = jnp.concatenate([mid_ref[dx, dy] for dy in range(3)], axis=1)
-            block = block + dot(lhs, rhs)
+            block = block + dot(mid_ref[dx], rhs)
+        block_ref[i] = block
+
+    def norm(i):
+        block = block_ref[i]
         center = jnp.mean(block, axis=0, keepdims=True)
         moved = block - center
         spread = jnp.mean(moved * moved, axis=0, keepdims=True)
         gain = jnp.concatenate([gain_ref[...]] * 2, axis=1)
-        normed = (moved * lax.rsqrt(spread + 1e-05) * gain).astype(BF16)
-        project = dot(qkvt_ref[...], normed)
-        mixed = []
+        normed_ref[i] = (moved * lax.rsqrt(spread + 1e-05) * gain).astype(BF16)
+
+    def project(i):
+        project_ref[i] = dot(qkvt_ref[...], normed_ref[i])
+
+    def units(i):
         for h in range(HEADS):
-            query = unit(project[h * HD : (h + 1) * HD], hs_ref[h] * math.log2(math.e))
-            key = unit(project[CH + h * HD : CH + (h + 1) * HD], 1.0)
-            value = project[2 * CH + h * HD : 2 * CH + (h + 1) * HD].astype(BF16)
-            value = jnp.concatenate([value, jnp.ones((16, 2 * FR), BF16)], axis=0)
-            parts = []
+            at = h * HD
+            unit_ref[i, at : at + HD] = unit(project_ref[i, at : at + HD], hs_ref[h] * math.log2(math.e))
+            at = CH + h * HD
+            unit_ref[i, at : at + HD] = unit(project_ref[i, at : at + HD], 1.0)
+            at = 2 * CH + h * HD
+            unit_ref[i, at : at + HD] = project_ref[i, at : at + HD].astype(BF16)
+
+    def turn_keys(i):
+        key_ref[i] = unit_ref[i, CH : 2 * CH].T
+
+    def attend(i):
+        for h in range(HEADS):
             for s in range(2):
                 cut = slice(s * FR, (s + 1) * FR)
-                scores = dot_t(key[:, cut], query[:, cut])
-                weights = jnp.exp2(scores).astype(BF16) * near_ref[...]
-                total = dot(value[:, cut], weights)
-                parts.append((total[:HD] / total[HD : HD + 1]).astype(BF16))
-            mixed.append(jnp.concatenate(parts, axis=1))
-        upper = block + dot(wot_ref[...], jnp.concatenate(mixed, axis=0))
-        noise_ref[i] = dot(wet_ref[...], silu(upper).astype(BF16))[:8]
-        return carry
-
-    lax.fori_loop(0, PX, body, 0)
+                scores = dot(key_ref[i, cut, h * HD : (h + 1) * HD], unit_ref[i, h * HD : (h + 1) * HD, cut])
+                weight_ref[i, 2 * h + s] = jnp.exp2(scores).astype(BF16) * near_ref[...]
+
+    def mix(i):
+        ones = jnp.ones((16, 2 * FR), BF16)
+        for h in range(HEADS):
+            at = 2 * CH + h * HD
+            value = jnp.concatenate([unit_ref[i, at : at + HD], ones], axis=0)
+            for s in range(2):
+                cut = slice(s * FR, (s + 1) * FR)
+                total = dot(value[:, cut], weight_ref[i, 2 * h + s])
+                mixed_ref[i, h * HD : (h + 1) * HD, cut] = (total[:HD] * (1.0 / total[HD : HD + 1])).astype(BF16)
+
+    def upper(i):
+        block_ref[i] = block_ref[i] + dot(wot_ref[...], mixed_ref[i])
+
+    def active(i):
+        normed_ref[i] = silu(block_ref[i]).astype(BF16)
+
+    def noise(i):
+        noise_ref[i] = dot(wet_ref[...], normed_ref[i])[:8]
+
+    for bodies in ((conv_mid, norm), (project, units, turn_keys), (attend,), (mix,), (upper, active), (noise,)):
+        each_pair(bodies)
 
 
 def advance(state, noise_ref, alpha, beta, entering):
@@ -257,6 +293,7 @@
            tw_ref, cmid_ref, qkv_ref, wo_ref, taps_ref,
            band_ref, mid_ref, qkvt_ref, wot_ref, wet_ref, gain_out, near_ref, ent_out,
            emb_ref, rhs_ref, hid_ref, act_ref, noise_ref,
+           block_ref, normed_ref, project_ref, unit_ref, key_ref, weight_ref, mixed_ref,
            send1, recv1, halo, own_ref, left_ref, right_ref, send3, recv3,
            load_sem, send1_sem, recv1_sem, send2_sem, recv2_sem, send3_sem, recv3_sem):
     q, t = lax.axis_index("queue"), lax.axis_index("tile")
@@ -322,7 +359,8 @@
     slots = [masked(slot[: 2 * ROW], i, q, t) for i, slot in enumerate(slots)]
 
     conv_in(slots, band_ref, emb_ref, rhs_ref, hid_ref, act_ref, q, t)
-    block_net(hs_ref, mid_ref, qkvt_ref, wot_ref, wet_ref, gain_out, near_ref, hid_ref, act_ref, noise_ref)
+    block_net(hs_ref, mid_ref, qkvt_ref, wot_ref, wet_ref, gain_out, near_ref, hid_ref, act_ref, noise_ref,
+              block_ref, normed_ref, project_ref, unit_ref, key_ref, weight_ref, mixed_ref)
     state = advance(state, noise_ref, alpha, beta, ent_out[0])
 
     own_ref[...] = state
@@ -352,7 +390,8 @@
     slots = [masked(halo[i], i, q, t) for i in range(3)]
 
     conv_in(slots, band_ref, emb_ref, rhs_ref, hid_ref, act_ref, q, t)
-    block_net(hs_ref, mid_ref, qkvt_ref, wot_ref, wet_ref, gain_out, near_ref, hid_ref, act_ref, noise_ref)
+    block_net(hs_ref, mid_ref, qkvt_ref, wot_ref, wet_ref, gain_out, near_ref, hid_ref, act_ref, noise_ref,
+              block_ref, normed_ref, project_ref, unit_ref, key_ref, weight_ref, mixed_ref)
     state = advance(own_ref[...], noise_ref, alpha, beta, ent_out[1])
 
     frames = jnp.concatenate([state, jnp.zeros((64, FR), F32)], axis=0).T
@@ -404,10 +443,13 @@
         out_specs=vmem,
         scratch_shapes=[
             v((CH, CH), F32), v((3, 3, CH, CH), BF16), v((CH, 3 * CH), BF16), v((CH, CH), BF16), v((40, CH), F32),
-            v((PX + 2, CH, TAPS), BF16), v((3, 3, CH, CH), BF16), v((3 * CH, CH), BF16), v((CH, CH), BF16),
+            v((PX + 2, CH, TAPS), BF16), v((3, CH, 3 * CH), BF16), v((3 * CH, CH), BF16), v((CH, CH), BF16),
             v((16, CH), BF16), v((CH, FR), F32), v((FR, FR), BF16), v((STEPS, 64, FR), F32),
             v((CH, FR), F32), v((2, TAPS, 2 * FR), BF16), v((PX + 2, 2, CH, FR), F32),
             v((PX + 2, 4, CH, FR), BF16), v((PX, 8, 2 * FR), F32),
+            v((PX, CH, 2 * FR), F32), v((PX, CH, 2 * FR), BF16), v((PX, 3 * CH, 2 * FR), F32),
+            v((PX, 3 * CH, 2 * FR), BF16), v((PX, 2 * FR, CH), BF16), v((PX, 2 * HEADS, FR, FR), BF16),
+            v((PX, CH, 2 * FR), BF16),
             v((NQ, 8, FR), F32), v((3, FR, FR), F32), v((3, 2 * ROW, FR), F32), v((64, FR), F32),
             v((16, FR), F32), v((16, FR), F32), v((NQ, 8, FR), F32), v((NQ, 8, FR), F32),
             dma((4,)), dma((3,)), dma((3,)), dma((8,)), dma((8,)), dma((1,)), dma((1,)),

time: 101 us -> 56.5 us (0.56)
  Pallas kernels: 97.1 us -> 52.1 us
    pallas_call x1, Pallas kernels: 97.1 us -> 52.1 us  [per_device(): pl.pallas_call(kernel, out_shape=jax.ShapeDtypeStruct(queue_latents.shape...]
where the time goes in v1:
time: 56.5 us; the launch traced here: 56.2 us
  Pallas kernels  52.1 us (92%)
  local copies, waits for them, and re-layouts  4.06 us (7%)
    pallas_call x1, Pallas kernels, per_device(): pl.pallas_call(kernel, out_shape=jax.ShapeDtypeStruct(queue_latents.shape...  52.1 us
    unnamed x2, local copies, waits for them, and re-layouts  2.82 us
    reshape x1, local copies, waits for them, and re-layouts, per_device(): norm_gain.reshape(1, CH)  1.24 us

profile of v1, /device:TPU:1, one launch (start us, length us, event | category | flops | bytes accessed | tf_op | source)
XLA Modules:
  0.0 56.2 jit_solution(13926646298947568459)
XLA Ops:
  0.0 1.2 %reshape.3.gain_ref = f32[1,320]{1,0:T(1,128)} reshape(f32[320]{0:T(512)} %param.17) | data formatting | bytes 2560 | tf_op jit(solution)/shard_map/reshape | solution.py:460
  1.2 1.4 %copy.12.we_ref = bf16[320,4]{1,0:T(8,128)(2,1)} copy(bf16[320,4]{0,1:T(4,128)(2,1)} %param.21) | data formatting | bytes 5120 | tf_op args[10]
  2.7 52.1 %shard_map.109 = f32[8,4,2,128]{3,2,1,0:T(2,128)} custom-call(f32[8,4,2,128]{3,2,1,0:T(2,128)} %lat_ref.1, f32[2,4,2,128]{3,2,1,0:T(2,128)} %ent_ref.1, s32[8]{0:T(128)} %lev_ref.1, f32[320,320]{1,0:T(8,128)} %tw_hbm.1, bf16[3,3,4,320]{3,2,1,0:T(4,128)(2,1)} %cin_ref.1, bf16[3,3,320,320]{3,2,1,0:T(8,128)(2,1)} %cmid_hbm.1, f32[1,320]{1,0:T(1,128)} %reshape.3.gain_ref, ...), custom_call_target="tpu_custom_call" | custom-call | tf_op jit(solution)/shard_map/pallas_call | solution.py:439
  54.8 1.4 %copy.14 = f32[8,4,2,128]{3,2,1,0:T(2,128)} copy(f32[8,4,2,128]{3,2,1,0:T(2,128)} %shard_map.109) | data formatting | bytes 65536

commit v2 on v1

--- a/solution.py
+++ b/solution.py
@@ -105,13 +105,14 @@
         dx = rel - w
         pick = (dx >= 0) & (dx <= 2) & (m == dy * 12 + dx * 4 + c)
         band_ref[w] = dot(taps_t, jnp.where(pick, 1.0, 0.0).astype(BF16)).astype(BF16)
-    for dx in range(3):
-        mid_ref[dx] = jnp.concatenate([cmid_ref[dy_, dx] for dy_ in range(3)], axis=0).T
+    taps = [jnp.concatenate([cmid_ref[dy, dx].astype(F32) for dx in range(3)], axis=0) for dy in range(3)]
+    outer = 0.5 * (taps[0] + taps[2])
+    for v, mid in enumerate((taps[0], outer + 0.5 * taps[1], outer - 0.5 * taps[1], taps[2])):
+        mid_ref[v] = mid.astype(BF16).T
     qkvt_ref[...] = qkv_ref[...].T
     wot_ref[...] = wo_ref[...].T
-    eps = jnp.concatenate([we_ref[...].astype(F32), jnp.zeros((CH, FR - 4), F32)], axis=1)
-    wet_ref[...] = eps.T[:16].astype(BF16)
-    gain_out[...] = jnp.broadcast_to(gain_ref[...], (FR, CH)).T
+    wet_ref[...] = jnp.concatenate([we_ref[...].astype(F32), jnp.zeros((12, CH), F32)], axis=0).astype(BF16)
+    gain_out[...] = jnp.broadcast_to(gain_ref[...].reshape(1, CH), (FR, CH)).T
     key_slot = lax.broadcasted_iota(jnp.int32, (FR, FR), 0)
     query_slot = lanes((FR, FR))
     near_ref[...] = jnp.where(jnp.abs(key_slot - query_slot) <= WIN, 1.0, 0.0).astype(BF16)
@@ -125,6 +126,19 @@
             ent_out[s, 8 * i : 8 * i + 8, :] = jnp.where(lane == FR - 1, shifted, 0.0)
 
 
+def blank(query_ref, value_ref, weight_ref):
+    def body(i, carry):
+        for p in range(5):
+            query_ref[i, p, :HD, FR:] = jnp.zeros((HD, FR), BF16)
+            query_ref[i, p, HD:, :FR] = jnp.zeros((HD, FR), BF16)
+            value_ref[i, p, HD:] = jnp.ones((16, 2 * FR), BF16)
+            weight_ref[i, p, :FR, FR:] = jnp.zeros((FR, FR), BF16)
+            weight_ref[i, p, FR:, :FR] = jnp.zeros((FR, FR), BF16)
+        return carry
+
+    lax.fori_loop(0, PX, body, 0)
+
+
 def embed(level, tw_ref, emb_ref):
     index = lax.broadcasted_iota(jnp.int32, (CH // 2, FR), 0).astype(F32)
     freqs = jnp.exp(-math.log(10000.0) * index / (CH // 2))
@@ -158,113 +172,102 @@
                 rows[2 * p + half : 2 * p + half + 3], axis=0)
 
     def body(w, carry):
+        inside = ((w > 0) | (q > 0)) & ((w < PX + 1) | (q < NQ - 1))
+        active = []
         for p in range(2):
             both = dot(band_ref[w], rhs_ref[p])
             for half in range(2):
                 hidden = both[:, half * FR : (half + 1) * FR] + emb_ref[...]
-                act_ref[w, 2 * p + half] = silu(hidden).astype(BF16)
                 if p != half:
                     hid_ref[w, p] = hidden
+                    active.append(jnp.where(inside, silu(hidden), 0.0))
+                else:
+                    active.append(jnp.where(inside & ((t > 0) if p == 0 else (t < NT - 1)), silu(hidden), 0.0))
+        a0, a1, a2, a3 = active
+        for v, part in enumerate((a0 - a2, a1 + a2, a2 - a1, a1 - a3)):
+            act_ref[w, v] = part.astype(BF16)
         return carry
 
     lax.fori_loop(0, PX + 2, body, 0, unroll=5)
-
-    @pl.when(t == 0)
-    def _():
-        for w in range(PX + 2):
-            act_ref[w, 0] = jnp.zeros((CH, FR), BF16)
-
-    @pl.when(t == NT - 1)
-    def _():
-        for w in range(PX + 2):
-            act_ref[w, 3] = jnp.zeros((CH, FR), BF16)
-
-    @pl.when(q == 0)
-    def _():
-        for r in range(4):
-            act_ref[0, r] = jnp.zeros((CH, FR), BF16)
-
-    @pl.when(q == NQ - 1)
-    def _():
-        for r in range(4):
-            act_ref[PX + 1, r] = jnp.zeros((CH, FR), BF16)
 
 
 def unit(x, scale):
     return (x * (lax.rsqrt(jnp.sum(x * x, axis=0, keepdims=True) + 1e-06) * scale)).astype(BF16)
 
 
-def each_pair(bodies):
+def each(bodies, count):
     def step(i, carry):
         for body in bodies:
             body(i)
         return carry
 
-    lax.fori_loop(0, PX, step, 0, unroll=PX)
+    lax.fori_loop(0, count, step, 0, unroll=count)
+
+
+def places():
+    pairs = [((s, 2 * p), (s, 2 * p + 1)) for s in range(2) for p in range(2)]
+    return pairs + [((0, 4), (1, 4))]
 
 
 def block_net(hs_ref, mid_ref, qkvt_ref, wot_ref, wet_ref, gain_ref, near_ref, hid_ref, act_ref, noise_ref,
-              block_ref, normed_ref, project_ref, unit_ref, key_ref, weight_ref, mixed_ref):
-    def conv_mid(i):
-        r, j = lax.div(i, 4), lax.rem(i, 4)
-        block = jnp.concatenate([hid_ref[2 * j + 1, r], hid_ref[2 * j + 2, r]], axis=1)
-        for dx in range(3):
-            rhs = jnp.concatenate(
-                [act_ref[2 * j + dx + s, pl.ds(r, 3)].reshape(3 * CH, FR) for s in range(2)], axis=1)
-            block = block + dot(mid_ref[dx], rhs)
+              block_ref, normed_ref, project_ref, query_ref, stack_ref, key_ref, value_ref, weight_ref, mixed_ref):
+    def norm(i, block):
         block_ref[i] = block
-
-    def norm(i):
-        block = block_ref[i]
         center = jnp.mean(block, axis=0, keepdims=True)
         moved = block - center
         spread = jnp.mean(moved * moved, axis=0, keepdims=True)
         gain = jnp.concatenate([gain_ref[...]] * 2, axis=1)
         normed_ref[i] = (moved * lax.rsqrt(spread + 1e-05) * gain).astype(BF16)
 
+    def conv_mid(j):
+        parts = []
+        for v in range(4):
+            rhs = [jnp.concatenate([act_ref[2 * j + dx, v], act_ref[2 * j + dx + 1, v]], axis=1) for dx in range(3)]
+            parts.append(dot(mid_ref[v], jnp.concatenate(rhs, axis=0)))
+        for r, part in enumerate((parts[0] + (parts[1] + parts[2]), (parts[1] - parts[2]) - parts[3])):
+            hidden = jnp.concatenate([hid_ref[2 * j + 1, r], hid_ref[2 * j + 2, r]], axis=1)
+            norm(4 * r + j, hidden + part)
+
     def project(i):
         project_ref[i] = dot(qkvt_ref[...], normed_ref[i])
 
     def units(i):
-        for h in range(HEADS):
-            at = h * HD
-            unit_ref[i, at : at + HD] = unit(project_ref[i, at : at + HD], hs_ref[h] * math.log2(math.e))
-            at = CH + h * HD
-            unit_ref[i, at : at + HD] = unit(project_ref[i, at : at + HD], 1.0)
-            at = 2 * CH + h * HD
-            unit_ref[i, at : at + HD] = project_ref[i, at : at + HD].astype(BF16)
-
-    def turn_keys(i):
-        key_ref[i] = unit_ref[i, CH : 2 * CH].T
+        for p, pair in enumerate(places()):
+            for n, (s, h) in enumerate(pair):
+                cut, own = slice(s * FR, (s + 1) * FR), slice(n * FR, (n + 1) * FR)
+                part = lambda k: project_ref[i, k * CH + h * HD : k * CH + (h + 1) * HD, cut]
+                query_ref[i, p, n * HD : (n + 1) * HD, own] = unit(part(0), hs_ref[h] * math.log2(math.e))
+                stack_ref[i, p, n * HD : (n + 1) * HD] = unit(part(1), 1.0)
+                value_ref[i, p, :HD, own] = part(2).astype(BF16)
+            key_ref[i, p] = stack_ref[i, p].T
 
     def attend(i):
-        for h in range(HEADS):
-            for s in range(2):
+        for p in range(5):
+            weights = jnp.exp2(dot(key_ref[i, p], query_ref[i, p])).astype(BF16)
+            for n in range(2):
+                own = slice(n * FR, (n + 1) * FR)
+                weight_ref[i, p, own, own] = weights[:, own] * near_ref[...]
+
+    def mix(i):
+        for p, ((s, h), _) in enumerate(places()):
+            total = dot(value_ref[i, p], weight_ref[i, p])
+            part = (total[:HD] * (1.0 / total[HD : HD + 1])).astype(BF16)
+            if p == 4:
+                mixed_ref[i, h * HD :, :] = part
+            else:
                 cut = slice(s * FR, (s + 1) * FR)
-                scores = dot(key_ref[i, cut, h * HD : (h + 1) * HD], unit_ref[i, h * HD : (h + 1) * HD, cut])
-                weight_ref[i, 2 * h + s] = jnp.exp2(scores).astype(BF16) * near_ref[...]
-
-    def mix(i):
-        ones = jnp.ones((16, 2 * FR), BF16)
-        for h in range(HEADS):
-            at = 2 * CH + h * HD
-            value = jnp.concatenate([unit_ref[i, at : at + HD], ones], axis=0)
-            for s in range(2):
-                cut = slice(s * FR, (s + 1) * FR)
-                total = dot(value[:, cut], weight_ref[i, 2 * h + s])
-                mixed_ref[i, h * HD : (h + 1) * HD, cut] = (total[:HD] * (1.0 / total[HD : HD + 1])).astype(BF16)
+                mixed_ref[i, h * HD : (h + 1) * HD, cut] = part[:, :FR]
+                mixed_ref[i, (h + 1) * HD : (h + 2) * HD, cut] = part[:, FR:]
 
     def upper(i):
-        block_ref[i] = block_ref[i] + dot(wot_ref[...], mixed_ref[i])
-
-    def active(i):
-        normed_ref[i] = silu(block_ref[i]).astype(BF16)
+        normed_ref[i] = silu(block_ref[i] + dot(wot_ref[...], mixed_ref[i])).astype(BF16)
 
     def noise(i):
         noise_ref[i] = dot(wet_ref[...], normed_ref[i])[:8]
 
-    for bodies in ((conv_mid, norm), (project, units, turn_keys), (attend,), (mix,), (upper, active), (noise,)):
-        each_pair(bodies)
+    each((conv_mid,), PX // 2)
+    for bodies in ((project, units), (attend,), (mix,), (upper,), (noise,)):
+        each(bodies, PX)
 
 
 def advance(state, noise_ref, alpha, beta, entering):
@@ -293,7 +296,7 @@
            tw_ref, cmid_ref, qkv_ref, wo_ref, taps_ref,
            band_ref, mid_ref, qkvt_ref, wot_ref, wet_ref, gain_out, near_ref, ent_out,
            emb_ref, rhs_ref, hid_ref, act_ref, noise_ref,
-           block_ref, normed_ref, project_ref, unit_ref, key_ref, weight_ref, mixed_ref,
+           block_ref, normed_ref, project_ref, query_ref, stack_ref, key_ref, value_ref, weight_ref, mixed_ref,
            send1, recv1, halo, own_ref, left_ref, right_ref, send3, recv3,
            load_sem, send1_sem, recv1_sem, send2_sem, recv2_sem, send3_sem, recv3_sem):
     q, t = lax.axis_index("queue"), lax.axis_index("tile")
@@ -346,6 +349,8 @@
         load.wait()
     prepare(cin_ref, cmid_ref, gain_ref, qkv_ref, wo_ref, we_ref, ent_ref, taps_ref,
             band_ref, mid_ref, qkvt_ref, wot_ref, wet_ref, gain_out, near_ref, ent_out, q)
+
+    blank(query_ref, value_ref, weight_ref)
 
     for slot in range(3):
         count = FR if slot != 1 else FR - 8
@@ -360,7 +365,7 @@
 
     conv_in(slots, band_ref, emb_ref, rhs_ref, hid_ref, act_ref, q, t)
     block_net(hs_ref, mid_ref, qkvt_ref, wot_ref, wet_ref, gain_out, near_ref, hid_ref, act_ref, noise_ref,
-              block_ref, normed_ref, project_ref, unit_ref, key_ref, weight_ref, mixed_ref)
+              block_ref, normed_ref, project_ref, query_ref, stack_ref, key_ref, value_ref, weight_ref, mixed_ref)
     state = advance(state, noise_ref, alpha, beta, ent_out[0])
 
     own_ref[...] = state
@@ -391,7 +396,7 @@
 
     conv_in(slots, band_ref, emb_ref, rhs_ref, hid_ref, act_ref, q, t)
     block_net(hs_ref, mid_ref, qkvt_ref, wot_ref, wet_ref, gain_out, near_ref, hid_ref, act_ref, noise_ref,
-              block_ref, normed_ref, project_ref, unit_ref, key_ref, weight_ref, mixed_ref)
+              block_ref, normed_ref, project_ref, query_ref, stack_ref, key_ref, value_ref, weight_ref, mixed_ref)
     state = advance(own_ref[...], noise_ref, alpha, beta, ent_out[1])
 
     frames = jnp.concatenate([state, jnp.zeros((64, FR), F32)], axis=0).T
@@ -443,13 +448,13 @@
         out_specs=vmem,
         scratch_shapes=[
             v((CH, CH), F32), v((3, 3, CH, CH), BF16), v((CH, 3 * CH), BF16), v((CH, CH), BF16), v((40, CH), F32),
-            v((PX + 2, CH, TAPS), BF16), v((3, CH, 3 * CH), BF16), v((3 * CH, CH), BF16), v((CH, CH), BF16),
+            v((PX + 2, CH, TAPS), BF16), v((4, CH, 3 * CH), BF16), v((3 * CH, CH), BF16), v((CH, CH), BF16),
             v((16, CH), BF16), v((CH, FR), F32), v((FR, FR), BF16), v((STEPS, 64, FR), F32),
             v((CH, FR), F32), v((2, TAPS, 2 * FR), BF16), v((PX + 2, 2, CH, FR), F32),
             v((PX + 2, 4, CH, FR), BF16), v((PX, 8, 2 * FR), F32),
             v((PX, CH, 2 * FR), F32), v((PX, CH, 2 * FR), BF16), v((PX, 3 * CH, 2 * FR), F32),
-            v((PX, 3 * CH, 2 * FR), BF16), v((PX, 2 * FR, CH), BF16), v((PX, 2 * HEADS, FR, FR), BF16),
-            v((PX, CH, 2 * FR), BF16),
+            v((PX, 5, FR, 2 * FR), BF16), v((PX, 5, FR, FR), BF16), v((PX, 5, FR, FR), BF16),
+            v((PX, 5, HD + 16, 2 * FR), BF16), v((PX, 5, 2 * FR, 2 * FR), BF16), v((PX, CH, 2 * FR), BF16),
             v((NQ, 8, FR), F32), v((3, FR, FR), F32), v((3, 2 * ROW, FR), F32), v((64, FR), F32),
             v((16, FR), F32), v((16, FR), F32), v((NQ, 8, FR), F32), v((NQ, 8, FR), F32),
             dma((4,)), dma((3,)), dma((3,)), dma((8,)), dma((8,)), dma((1,)), dma((1,)),
@@ -457,7 +462,7 @@
         compiler_params=pltpu.CompilerParams(
             collective_id=0, has_side_effects=True, vmem_limit_bytes=56 * 1024 * 1024),
     )(queue_latents, entering, levels, time_weight, conv_in_weight, conv_mid_weight,
-      norm_gain.reshape(1, CH), qkv_weight, head_scale, attn_out_weight, eps_out_weight)
+      norm_gain, qkv_weight, head_scale, attn_out_weight, eps_out_weight.T)
 
 
 def solution(mesh):

time: 56.5 us -> 52.1 us (0.922)
  local copies, waits for them, and re-layouts: 4.06 us -> 1.38 us
  Pallas kernels: 52.1 us -> 50.5 us
    pallas_call x1, Pallas kernels: 52.1 us -> 50.5 us  [per_device(): pl.pallas_call(kernel, out_shape=jax.ShapeDtypeStruct(queue_latents.shape...]
    unnamed x2 -> x1, local copies, waits for them, and re-layouts: 2.82 us -> 1.38 us
    reshape x1 -> x0, local copies, waits for them, and re-layouts: 1.24 us -> none  [per_device(): norm_gain.reshape(1, CH)]
where the time goes in v2:
time: 52.1 us; the launch traced here: 51.9 us
  Pallas kernels  50.5 us (97%)
  local copies, waits for them, and re-layouts  1.38 us (3%)
    pallas_call x1, Pallas kernels, per_device(): pl.pallas_call(kernel, out_shape=jax.ShapeDtypeStruct(queue_latents.shape...  50.5 us
    unnamed x1, local copies, waits for them, and re-layouts  1.38 us

profile of v2, /device:TPU:1, one launch (start us, length us, event | category | flops | bytes accessed | tf_op | source)
XLA Modules:
  0.0 51.9 jit_solution(15818605939584476825)
XLA Ops:
  0.0 50.5 %shard_map.109 = f32[8,4,2,128]{3,2,1,0:T(2,128)} custom-call(f32[8,4,2,128]{3,2,1,0:T(2,128)} %lat_ref.1, f32[2,4,2,128]{3,2,1,0:T(2,128)} %ent_ref.1, s32[8]{0:T(128)} %lev_ref.1, f32[320,320]{1,0:T(8,128)} %tw_hbm.1, bf16[3,3,4,320]{3,2,1,0:T(4,128)(2,1)} %cin_ref.1, bf16[3,3,320,320]{3,2,1,0:T(8,128)(2,1)} %cmid_hbm.1, f32[320]{0:T(512)} %gain_ref.1, ...), custom_call_target="tpu_custom_call" | custom-call | tf_op jit(solution)/shard_map/pallas_call | solution.py:444
  50.5 1.4 %copy.13 = f32[8,4,2,128]{3,2,1,0:T(2,128)} copy(f32[8,4,2,128]{3,2,1,0:T(2,128)} %shard_map.109) | data formatting | bytes 65536

commit v3 on v2

--- a/solution.py
+++ b/solution.py
@@ -60,6 +60,19 @@
     return lax.broadcasted_iota(jnp.int32, shape, 1)
 
 
+OFFSETS = sorted(((z, x, c) for z in (0, 1) for x in range(4) for c in (0, 1)),
+                 key=lambda o: -(2 * o[0] + min(o[1], 4 - o[1]) + 0.1 * o[2]))
+
+
+def peer_at(q, offset):
+    z, x, c = offset
+    return ((q // 8 + z) % 2) * 8 + ((q // 2 + x) % 4) * 2 + (q + c) % 2
+
+
+def group_of(q):
+    return jnp.where(q < NQ // 2, q, 3 * NQ // 2 - 1 - q)
+
+
 def pack_latents(lat_ref, lev_ref, send_ref):
     lane = lanes((8, FR))
     row = lax.broadcasted_iota(jnp.int32, (8, FR), 0)
@@ -87,8 +100,8 @@
     lax.fori_loop(0, NQ, body, 0)
 
 
-def prepare(cin_ref, cmid_ref, gain_ref, qkv_ref, wo_ref, we_ref, ent_ref, taps_ref,
-            band_ref, mid_ref, qkvt_ref, wot_ref, wet_ref, gain_out, near_ref, ent_out, q):
+def prepare(cin_ref, cmid_ref, gain_ref, qkv_ref, wo_ref, we_ref, ent_ref, tw_ref, taps_ref,
+            twt_ref, band_ref, mid_ref, qkvt_ref, wot_ref, wet_ref, gain_out, near_ref, ent_out, g):
     taps_ref[...] = jnp.zeros(taps_ref.shape, F32)
     for i in range(9):
         taps_ref[4 * i : 4 * i + 4, :] = cin_ref[i // 3, i % 3].astype(F32)
@@ -109,6 +122,10 @@
     outer = 0.5 * (taps[0] + taps[2])
     for v, mid in enumerate((taps[0], outer + 0.5 * taps[1], outer - 0.5 * taps[1], taps[2])):
         mid_ref[v] = mid.astype(BF16).T
+    weight = tw_ref[...].T
+    high = weight.astype(BF16)
+    low = (weight - high.astype(F32)).astype(BF16)
+    twt_ref[...] = jnp.concatenate([high, high, low], axis=1)
     qkvt_ref[...] = qkv_ref[...].T
     wot_ref[...] = wo_ref[...].T
     wet_ref[...] = jnp.concatenate([we_ref[...].astype(F32), jnp.zeros((12, CH), F32)], axis=0).astype(BF16)
@@ -119,7 +136,7 @@
     lane = lanes((8, FR))
     for s in range(STEPS):
         rows = jnp.concatenate([ent_ref[s, c, r : r + 1, :] for c in range(4) for r in range(2)], axis=0)
-        rows = pltpu.roll(rows, lax.rem(FR - 8 * q, FR), 1)
+        rows = pltpu.roll(rows, lax.rem(FR - 8 * g, FR), 1)
         columns = jnp.concatenate([rows, jnp.zeros((FR - 8, FR), F32)], axis=0).T[:8]
         for i in range(8):
             shifted = pltpu.roll(columns, FR - 1 - i, 1)
@@ -139,14 +156,14 @@
     lax.fori_loop(0, PX, body, 0)
 
 
-def embed(level, tw_ref, emb_ref):
+def embed(level, twt_ref, emb_ref):
     index = lax.broadcasted_iota(jnp.int32, (CH // 2, FR), 0).astype(F32)
     freqs = jnp.exp(-math.log(10000.0) * index / (CH // 2))
     sine, cosine = sin_cos(level * freqs)
     feature = jnp.concatenate([sine, cosine], axis=0)
-    emb_ref[...] = lax.dot_general(
-        tw_ref[...].T, feature, (((1,), (0,)), ((), ())),
-        precision=lax.Precision.HIGHEST, preferred_element_type=F32)
+    high = feature.astype(BF16)
+    low = (feature - high.astype(F32)).astype(BF16)
+    emb_ref[...] = dot(twt_ref[...], jnp.concatenate([high, low, high], axis=0))
 
 
 def coefficients(level):
@@ -160,19 +177,19 @@
     return alpha, s1 - alpha * s0
 
 
-def conv_in(slots, band_ref, emb_ref, rhs_ref, hid_ref, act_ref, q, t):
+def conv_in(slots, band_ref, emb_ref, rhs_ref, hid_ref, act_ref, g, t):
     rows = []
     for slot in slots:
         for r in range(2):
             rows.append(jnp.concatenate(
-                [slot[g * 16 + r * 8 : g * 16 + r * 8 + 8] for g in range(6)], axis=0).astype(BF16))
+                [slot[k * 16 + r * 8 : k * 16 + r * 8 + 8] for k in range(6)], axis=0).astype(BF16))
     for p in range(2):
         for half in range(2):
             rhs_ref[p, :, half * FR : (half + 1) * FR] = jnp.concatenate(
                 rows[2 * p + half : 2 * p + half + 3], axis=0)
 
     def body(w, carry):
-        inside = ((w > 0) | (q > 0)) & ((w < PX + 1) | (q < NQ - 1))
+        inside = ((w > 0) | (g > 0)) & ((w < PX + 1) | (g < NQ - 1))
         active = []
         for p in range(2):
             both = dot(band_ref[w], rhs_ref[p])
@@ -188,7 +205,7 @@
             act_ref[w, v] = part.astype(BF16)
         return carry
 
-    lax.fori_loop(0, PX + 2, body, 0, unroll=5)
+    lax.fori_loop(0, PX + 2, body, 0, unroll=PX + 2)
 
 
 def unit(x, scale):
@@ -282,172 +299,178 @@
     return jnp.where(lanes((64, FR)) == FR - 1, entering, pltpu.roll(updated, FR - 1, 1))
 
 
-def masked(slot, index, q, t):
+def masked(slot, index, g, t):
     inside = (t > 0) if index == 0 else (t < NT - 1) if index == 2 else None
     own, left, right = slot[:64], slot[64:80], slot[80:96]
-    left = jnp.where(q > 0, left, 0.0)
-    right = jnp.where(q < NQ - 1, right, 0.0)
+    left = jnp.where(g > 0, left, 0.0)
+    right = jnp.where(g < NQ - 1, right, 0.0)
     slot = jnp.concatenate([own, left, right], axis=0)
     return slot if inside is None else jnp.where(inside, slot, 0.0)
 
 
-def kernel(lat_ref, ent_ref, lev_ref, tw_hbm, cin_ref, cmid_hbm, gain_ref, qkv_hbm, hs_ref, wo_hbm, we_ref,
+def kernel(lat_hbm, ent_hbm, lev_hbm, tw_hbm, cin_hbm, cmid_hbm, gain_hbm, qkv_hbm, hs_hbm, wo_hbm, we_hbm,
            out_ref,
-           tw_ref, cmid_ref, qkv_ref, wo_ref, taps_ref,
-           band_ref, mid_ref, qkvt_ref, wot_ref, wet_ref, gain_out, near_ref, ent_out,
+           lat_ref, ent_ref, lev_ref, tw_ref, cin_ref, cmid_ref, gain_ref, qkv_ref, hs_ref, wo_ref, we_ref, taps_ref,
+           twt_ref, band_ref, mid_ref, qkvt_ref, wot_ref, wet_ref, gain_out, near_ref, ent_out,
            emb_ref, rhs_ref, hid_ref, act_ref, noise_ref,
            block_ref, normed_ref, project_ref, query_ref, stack_ref, key_ref, value_ref, weight_ref, mixed_ref,
-           send1, recv1, halo, own_ref, left_ref, right_ref, send3, recv3,
+           send1, recv1, halo, state_ref, own_ref, left_ref, right_ref, send3, recv3,
            load_sem, send1_sem, recv1_sem, send2_sem, recv2_sem, send3_sem, recv3_sem):
     q, t = lax.axis_index("queue"), lax.axis_index("tile")
+    g = group_of(q)
+    sides = [(t > 0, t - 1, 2), (t < NT - 1, t + 1, 0)]
+    others = OFFSETS[:-1]
+
+    barrier = pltpu.get_barrier_semaphore()
+    for there, row, _ in sides:
+        @pl.when(there)
+        def _():
+            for offset in OFFSETS:
+                pl.semaphore_signal(barrier, inc=1, device_id=(peer_at(q, offset), row), device_id_type=MESH)
+    for offset in others:
+        pl.semaphore_signal(barrier, inc=1, device_id=(peer_at(q, offset), t), device_id_type=MESH)
+
     loads = [pltpu.make_async_copy(src, dst, load_sem.at[i]) for i, (src, dst) in enumerate(
-        [(cmid_hbm, cmid_ref), (qkv_hbm, qkv_ref), (wo_hbm, wo_ref), (tw_hbm, tw_ref)])]
+        [(lat_hbm, lat_ref), (lev_hbm, lev_ref), (cmid_hbm, cmid_ref), (qkv_hbm, qkv_ref), (wo_hbm, wo_ref),
+         (tw_hbm, tw_ref), (ent_hbm, ent_ref), (cin_hbm, cin_ref), (gain_hbm, gain_ref), (hs_hbm, hs_ref),
+         (we_hbm, we_ref)])]
     for load in loads:
         load.start()
-
-    barrier = pltpu.get_barrier_semaphore()
-    above, below = lax.rem(t + NT - 1, NT), lax.rem(t + 1, NT)
-
-    def greet(k, carry):
-        peer = lax.rem(q + k, NQ)
-        pl.semaphore_signal(barrier, inc=1, device_id=(peer, above), device_id_type=MESH)
-        pl.semaphore_signal(barrier, inc=1, device_id=(peer, below), device_id_type=MESH)
-        return carry
-
-    def greet_row(k, carry):
-        pl.semaphore_signal(barrier, inc=1, device_id=(lax.rem(q + k, NQ), t), device_id_type=MESH)
-        return carry
-
-    lax.fori_loop(0, NQ, greet, 0)
-    lax.fori_loop(1, NQ, greet_row, 0)
+    for load in loads[:2]:
+        load.wait()
     pack_latents(lat_ref, lev_ref, send1)
-    pl.semaphore_wait(barrier, 3 * NQ - 1)
+    both = (t > 0).astype(jnp.int32) + (t < NT - 1).astype(jnp.int32)
+    pl.semaphore_wait(barrier, NQ - 1 + NQ * both)
 
     place = pl.ds(pl.multiple_of(q * 8, 8), 8)
 
-    def to_peer(peer, row, slot):
+    def to_peer(offset, row, slot):
+        peer = peer_at(q, offset)
         pltpu.make_async_remote_copy(
-            src_ref=send1.at[peer], dst_ref=recv1.at[slot, place],
+            src_ref=send1.at[group_of(peer)], dst_ref=recv1.at[slot, place],
             send_sem=send1_sem.at[slot], recv_sem=recv1_sem.at[slot],
             device_id=(peer, row), device_id_type=MESH).start()
 
-    def scatter_row(k, carry):
-        to_peer(lax.rem(q + k, NQ), t, 1)
-        return carry
-
-    def scatter(k, carry):
-        peer = lax.rem(q + k, NQ)
-        to_peer(peer, above, 2)
-        to_peer(peer, below, 0)
-        return carry
-
-    lax.fori_loop(1, NQ, scatter_row, 0)
-    lax.fori_loop(0, NQ, scatter, 0)
-    recv1[1, place] = send1[q]
-
-    for load in loads:
+    for there, row, slot in sides:
+        @pl.when(there)
+        def _():
+            for offset in OFFSETS:
+                to_peer(offset, row, slot)
+    for offset in others:
+        to_peer(offset, t, 1)
+    recv1[1, place] = send1[g]
+
+    for load in loads[2:]:
         load.wait()
-    prepare(cin_ref, cmid_ref, gain_ref, qkv_ref, wo_ref, we_ref, ent_ref, taps_ref,
-            band_ref, mid_ref, qkvt_ref, wot_ref, wet_ref, gain_out, near_ref, ent_out, q)
-
+    prepare(cin_ref, cmid_ref, gain_ref, qkv_ref, wo_ref, we_ref, ent_ref, tw_ref, taps_ref,
+            twt_ref, band_ref, mid_ref, qkvt_ref, wot_ref, wet_ref, gain_out, near_ref, ent_out, g)
     blank(query_ref, value_ref, weight_ref)
 
-    for slot in range(3):
-        count = FR if slot != 1 else FR - 8
-        part = recv1.at[slot, pl.ds(0, count)]
-        pltpu.make_async_copy(part, part, recv1_sem.at[slot]).wait()
+    def settle(ref, sem, count):
+        part = ref.at[pl.ds(0, count)]
+        pltpu.make_async_copy(part, part, sem).wait()
+
+    settle(recv1.at[1], recv1_sem.at[1], FR - 8)
+    for there, slot in ((t > 0, 0), (t < NT - 1, 2)):
+        @pl.when(there)
+        def _():
+            settle(recv1.at[slot], recv1_sem.at[slot], FR)
     slots = [recv1[slot].T for slot in range(3)]
     level = slots[1][2 * ROW : 2 * ROW + 1]
-    embed(level, tw_ref, emb_ref)
+    embed(level, twt_ref, emb_ref)
     alpha, beta = coefficients(level)
     state = slots[1][:64]
-    slots = [masked(slot[: 2 * ROW], i, q, t) for i, slot in enumerate(slots)]
-
-    conv_in(slots, band_ref, emb_ref, rhs_ref, hid_ref, act_ref, q, t)
+    slots = [masked(slot[: 2 * ROW], i, g, t) for i, slot in enumerate(slots)]
+
+    conv_in(slots, band_ref, emb_ref, rhs_ref, hid_ref, act_ref, g, t)
     block_net(hs_ref, mid_ref, qkvt_ref, wot_ref, wet_ref, gain_out, near_ref, hid_ref, act_ref, noise_ref,
               block_ref, normed_ref, project_ref, query_ref, stack_ref, key_ref, value_ref, weight_ref, mixed_ref)
     state = advance(state, noise_ref, alpha, beta, ent_out[0])
 
-    own_ref[...] = state
+    state_ref[...] = state
+    own_ref[...] = state.astype(BF16)
+    lefts, rights = [], []
     for r in range(2):
         for c in range(4):
             at = c * 16 + r * 8
-            left_ref[r * 8 + c * 2 : r * 8 + c * 2 + 2, :] = state[at + 6 : at + 8]
-            right_ref[r * 8 + c * 2 : r * 8 + c * 2 + 2, :] = state[at : at + 2]
-    before, after = lax.rem(q + NQ - 1, NQ), lax.rem(q + 1, NQ)
+            lefts.append(state[at + 6 : at + 8])
+            rights.append(state[at : at + 2])
+    left_ref[...] = jnp.concatenate(lefts, axis=0).astype(BF16)
+    right_ref[...] = jnp.concatenate(rights, axis=0).astype(BF16)
     copies = []
-    for row, slot in ((t, 1), (above, 2), (below, 0)):
-        if slot != 1:
-            copies.append((own_ref, (0, 64), q, row, slot))
-        copies.append((left_ref, (64, 16), after, row, slot))
-        copies.append((right_ref, (80, 16), before, row, slot))
-    copies = [
-        pltpu.make_async_remote_copy(
-            src_ref=src, dst_ref=halo.at[slot, pl.ds(start, size)],
-            send_sem=send2_sem.at[i], recv_sem=recv2_sem.at[i],
-            device_id=(peer, row), device_id_type=MESH)
-        for i, (src, (start, size), peer, row, slot) in enumerate(copies)]
-    for copy in copies:
-        copy.start()
-    for copy in copies:
-        copy.wait_recv()
+    for src, start, size, step in ((left_ref, 64, 16, 1), (right_ref, 80, 16, -1), (own_ref, 0, 64, 0)):
+        sent, got = (g < NQ - 1, g > 0) if step == 1 else (g > 0, g < NQ - 1) if step == -1 else (None, None)
+        peer = group_of(jnp.clip(g + step, 0, NQ - 1))
+        for down in (-1, 1, 0):
+            if step == 0 and down == 0:
+                continue
+            sent_too, got_too = (t > 0, t < NT - 1) if down == -1 else (t < NT - 1, t > 0) if down == 1 else (None, None)
+            both_of = lambda a, b: b if a is None else a if b is None else a & b
+            i = len(copies)
+            copies.append((both_of(sent, sent_too), both_of(got, got_too), pltpu.make_async_remote_copy(
+                src_ref=src, dst_ref=halo.at[1 - down, pl.ds(start, size)],
+                send_sem=send2_sem.at[i], recv_sem=recv2_sem.at[i],
+                device_id=(peer, t + down), device_id_type=MESH)))
+    for sent, _, copy in copies:
+        pl.when(sent)(copy.start)
+    for _, got, copy in copies:
+        pl.when(got)(copy.wait_recv)
     halo[1, :64] = own_ref[...]
-    slots = [masked(halo[i], i, q, t) for i in range(3)]
-
-    conv_in(slots, band_ref, emb_ref, rhs_ref, hid_ref, act_ref, q, t)
+    slots = [masked(halo[i].astype(F32), i, g, t) for i in range(3)]
+
+    conv_in(slots, band_ref, emb_ref, rhs_ref, hid_ref, act_ref, g, t)
     block_net(hs_ref, mid_ref, qkvt_ref, wot_ref, wet_ref, gain_out, near_ref, hid_ref, act_ref, noise_ref,
               block_ref, normed_ref, project_ref, query_ref, stack_ref, key_ref, value_ref, weight_ref, mixed_ref)
-    state = advance(own_ref[...], noise_ref, alpha, beta, ent_out[1])
+    state = advance(state_ref[...], noise_ref, alpha, beta, ent_out[1])
 
     frames = jnp.concatenate([state, jnp.zeros((64, FR), F32)], axis=0).T
     for peer in range(NQ):
         send3[peer] = frames[peer * 8 : peer * 8 + 8]
-
-    def give(k, carry):
-        peer = lax.rem(q + k, NQ)
+    for offset in others:
+        peer = peer_at(q, offset)
         pltpu.make_async_remote_copy(
-            src_ref=send3.at[peer], dst_ref=recv3.at[q],
+            src_ref=send3.at[peer], dst_ref=recv3.at[g],
             send_sem=send3_sem.at[0], recv_sem=recv3_sem.at[0],
             device_id=(peer, t), device_id_type=MESH).start()
-        return carry
-
-    lax.fori_loop(1, NQ, give, 0)
-    recv3[q] = send3[q]
-    for copy in copies:
-        copy.wait_send()
-    for slot in range(3):
-        part = send1.at[pl.ds(0, NQ if slot != 1 else NQ - 1)]
-        pltpu.make_async_copy(part, part, send1_sem.at[slot]).wait()
-    part = recv3.at[pl.ds(0, NQ - 1)]
-    pltpu.make_async_copy(part, part, recv3_sem.at[0]).wait()
-    part = send3.at[pl.ds(0, NQ - 1)]
-    pltpu.make_async_copy(part, part, send3_sem.at[0]).wait()
-
-    lane = lanes((8, FR))
+    recv3[g] = send3[q]
+    for sent, _, copy in copies:
+        pl.when(sent)(copy.wait_send)
+    settle(send1, send1_sem.at[1], NQ - 1)
+    for there, _, slot in sides:
+        @pl.when(there)
+        def _():
+            settle(send1, send1_sem.at[slot], NQ)
+    settle(recv3, recv3_sem.at[0], NQ - 1)
+    settle(send3, send3_sem.at[0], NQ - 1)
+
+    group = lanes((8, FR)) >> 3
+    turned = [pltpu.roll(recv3[source], 8 * source, 1) for source in range(NQ)]
     for c in range(4):
         for r in range(2):
-            at = c * 16 + r * 8
-            total = jnp.zeros((8, FR), F32)
-            for source in range(NQ):
-                moved = pltpu.roll(recv3[source], (FR + 8 * source - at) % FR, 1)
-                total = jnp.where((lane >> 3) == source, moved, total)
-            out_ref[:, c, r, :] = total
+            at = c * 2 + r
+            total = turned[0]
+            for source in range(1, NQ):
+                total = jnp.where(group == (source + at) % NQ, turned[source], total)
+            out_ref[:, c, r, :] = pltpu.roll(total, (FR - 8 * at) % FR, 1)
 
 
 def per_device(queue_latents, entering, levels, time_weight, conv_in_weight, conv_mid_weight, norm_gain,
                qkv_weight, head_scale, attn_out_weight, eps_out_weight):
-    vmem = pl.BlockSpec(memory_space=pltpu.VMEM)
-    smem = pl.BlockSpec(memory_space=pltpu.SMEM)
     hbm = pl.BlockSpec(memory_space=pl.ANY)
     v = pltpu.VMEM
     dma = pltpu.SemaphoreType.DMA
+    inputs = (queue_latents, entering, levels, time_weight, conv_in_weight, conv_mid_weight,
+              norm_gain, qkv_weight, head_scale, attn_out_weight, eps_out_weight.T)
+    scalars = (levels, head_scale)
     return pl.pallas_call(
         kernel,
         out_shape=jax.ShapeDtypeStruct(queue_latents.shape, F32),
-        in_specs=[vmem, vmem, smem, hbm, vmem, hbm, vmem, hbm, smem, hbm, vmem],
-        out_specs=vmem,
+        in_specs=[hbm] * len(inputs),
+        out_specs=pl.BlockSpec(memory_space=pltpu.VMEM),
         scratch_shapes=[
-            v((CH, CH), F32), v((3, 3, CH, CH), BF16), v((CH, 3 * CH), BF16), v((CH, CH), BF16), v((40, CH), F32),
+            *[(pltpu.SMEM if any(x is y for y in scalars) else v)(x.shape, x.dtype) for x in inputs],
+            v((40, CH), F32),
+            v((CH, 3 * CH), BF16),
             v((PX + 2, CH, TAPS), BF16), v((4, CH, 3 * CH), BF16), v((3 * CH, CH), BF16), v((CH, CH), BF16),
             v((16, CH), BF16), v((CH, FR), F32), v((FR, FR), BF16), v((STEPS, 64, FR), F32),
             v((CH, FR), F32), v((2, TAPS, 2 * FR), BF16), v((PX + 2, 2, CH, FR), F32),
@@ -455,14 +478,13 @@
             v((PX, CH, 2 * FR), F32), v((PX, CH, 2 * FR), BF16), v((PX, 3 * CH, 2 * FR), F32),
             v((PX, 5, FR, 2 * FR), BF16), v((PX, 5, FR, FR), BF16), v((PX, 5, FR, FR), BF16),
             v((PX, 5, HD + 16, 2 * FR), BF16), v((PX, 5, 2 * FR, 2 * FR), BF16), v((PX, CH, 2 * FR), BF16),
-            v((NQ, 8, FR), F32), v((3, FR, FR), F32), v((3, 2 * ROW, FR), F32), v((64, FR), F32),
-            v((16, FR), F32), v((16, FR), F32), v((NQ, 8, FR), F32), v((NQ, 8, FR), F32),
-            dma((4,)), dma((3,)), dma((3,)), dma((8,)), dma((8,)), dma((1,)), dma((1,)),
+            v((NQ, 8, FR), F32), v((3, FR, FR), F32), v((3, 2 * ROW, FR), BF16), v((64, FR), F32), v((64, FR), BF16),
+            v((16, FR), BF16), v((16, FR), BF16), v((NQ, 8, FR), F32), v((NQ, 8, FR), F32),
+            dma((len(inputs),)), dma((3,)), dma((3,)), dma((8,)), dma((8,)), dma((1,)), dma((1,)),
         ],
         compiler_params=pltpu.CompilerParams(
             collective_id=0, has_side_effects=True, vmem_limit_bytes=56 * 1024 * 1024),
-    )(queue_latents, entering, levels, time_weight, conv_in_weight, conv_mid_weight,
-      norm_gain, qkv_weight, head_scale, attn_out_weight, eps_out_weight.T)
+    )(*inputs)
 
 
 def solution(mesh):

time: 52.1 us -> 45.4 us (0.87)
  Pallas kernels: 50.5 us -> 43.9 us
    pallas_call x1, Pallas kernels: 50.5 us -> 43.9 us  [per_device(): pl.pallas_call(kernel, out_shape=jax.ShapeDtypeStruct(queue_latents.shape...]
where the time goes in v3:
time: 45.4 us; the launch traced here: 45.3 us
  Pallas kernels  43.9 us (97%)
  local copies, waits for them, and re-layouts  1.38 us (3%)
    pallas_call x1, Pallas kernels, per_device(): pl.pallas_call(kernel, out_shape=jax.ShapeDtypeStruct(queue_latents.shape...  43.9 us
    unnamed x1, local copies, waits for them, and re-layouts  1.38 us

profile of v3, /device:TPU:1, one launch (start us, length us, event | category | flops | bytes accessed | tf_op | source)
XLA Modules:
  0.0 45.3 jit_solution(15838850141757910076)
XLA Ops:
  0.0 43.9 %shard_map.109 = f32[8,4,2,128]{3,2,1,0:T(2,128)} custom-call(f32[8,4,2,128]{3,2,1,0:T(2,128)} %lat_hbm.1, f32[2,4,2,128]{3,2,1,0:T(2,128)} %ent_hbm.1, s32[8]{0:T(128)} %lev_hbm.1, f32[320,320]{1,0:T(8,128)} %tw_hbm.1, bf16[3,3,4,320]{3,2,1,0:T(4,128)(2,1)} %cin_hbm.1, bf16[3,3,320,320]{3,2,1,0:T(8,128)(2,1)} %cmid_hbm.1, f32[320]{0:T(512)} %gain_hbm.1, ...), custom_call_target="tpu_custom_call" | custom-call | tf_op jit(solution)/shard_map/pallas_call | solution.py:465
  43.9 1.4 %copy.13 = f32[8,4,2,128]{3,2,1,0:T(2,128)} copy(f32[8,4,2,128]{3,2,1,0:T(2,128)} %shard_map.109) | data formatting | bytes 65536

commit v4 on v3

--- a/solution.py
+++ b/solution.py
@@ -66,7 +66,7 @@
 
 def peer_at(q, offset):
     z, x, c = offset
-    return ((q // 8 + z) % 2) * 8 + ((q // 2 + x) % 4) * 2 + (q + c) % 2
+    return ((q ^ (8 * z)) & 8) | ((q + 2 * x) & 6) | ((q ^ c) & 1)
 
 
 def group_of(q):
@@ -441,7 +441,6 @@
         def _():
             settle(send1, send1_sem.at[slot], NQ)
     settle(recv3, recv3_sem.at[0], NQ - 1)
-    settle(send3, send3_sem.at[0], NQ - 1)
 
     group = lanes((8, FR)) >> 3
     turned = [pltpu.roll(recv3[source], 8 * source, 1) for source in range(NQ)]
@@ -452,6 +451,7 @@
             for source in range(1, NQ):
                 total = jnp.where(group == (source + at) % NQ, turned[source], total)
             out_ref[:, c, r, :] = pltpu.roll(total, (FR - 8 * at) % FR, 1)
+    settle(send3, send3_sem.at[0], NQ - 1)
 
 
 def per_device(queue_latents, entering, levels, time_weight, conv_in_weight, conv_mid_weight, norm_gain,
@@ -464,7 +464,7 @@
     scalars = (levels, head_scale)
     return pl.pallas_call(
         kernel,
-        out_shape=jax.ShapeDtypeStruct(queue_latents.shape, F32),
+        out_shape=pltpu.VMEM(queue_latents.shape, F32),
         in_specs=[hbm] * len(inputs),
         out_specs=pl.BlockSpec(memory_space=pltpu.VMEM),
         scratch_shapes=[

time: 45.4 us -> 44 us (0.969)
  local copies, waits for them, and re-layouts: 1.38 us -> 0.62 us
  Pallas kernels: 43.9 us -> 43.3 us
    unnamed x1, local copies, waits for them, and re-layouts: 1.38 us -> 0.62 us
    pallas_call x1, Pallas kernels: 43.9 us -> 43.3 us  [per_device(): pl.pallas_call(kernel, out_shape=pltpu.VMEM(queue_latents.shape, F32), in...]
where the time goes in v4:
time: 44 us; the launch traced here: 43.9 us
  Pallas kernels  43.3 us (98%)
  local copies, waits for them, and re-layouts  0.62 us (1%)
    pallas_call x1, Pallas kernels, per_device(): pl.pallas_call(kernel, out_shape=pltpu.VMEM(queue_latents.shape, F32), in...  43.3 us

profile of v4, /device:TPU:1, one launch (start us, length us, event | category | flops | bytes accessed | tf_op | source)
XLA Modules:
  0.0 43.9 jit_solution(4877876671463927055)
XLA Ops:
  0.0 43.3 %shard_map.109 = f32[8,4,2,128]{3,2,1,0:T(2,128)S(1)} custom-call(f32[8,4,2,128]{3,2,1,0:T(2,128)} %lat_hbm.1, f32[2,4,2,128]{3,2,1,0:T(2,128)} %ent_hbm.1, s32[8]{0:T(128)} %lev_hbm.1, f32[320,320]{1,0:T(8,128)} %tw_hbm.1, bf16[3,3,4,320]{3,2,1,0:T(4,128)(2,1)} %cin_hbm.1, bf16[3,3,320,320]{3,2,1,0:T(8,128)(2,1)} %cmid_hbm.1, f32[320]{0:T(512)} %gain_hbm.1, ...), custom_call_target="tpu_custom_call" | custom-call | tf_op jit(solution)/shard_map/pallas_call | solution.py:465
  43.3 0.6 %copy.13 = f32[8,4,2,128]{3,2,1,0:T(2,128)} copy(f32[8,4,2,128]{3,2,1,0:T(2,128)S(1)} %shard_map.109) | data formatting | bytes 65536

commit v5 on v4

--- a/solution.py
+++ b/solution.py
@@ -51,8 +51,7 @@
     return sin_out, cos_out
 
 
-def silu(x):
-    half = 0.5 * x
+def silu_of_half(half):
     return half + half * jnp.tanh(half)
 
 
@@ -117,22 +116,22 @@
     for w in range(PX + 2):
         dx = rel - w
         pick = (dx >= 0) & (dx <= 2) & (m == dy * 12 + dx * 4 + c)
-        band_ref[w] = dot(taps_t, jnp.where(pick, 1.0, 0.0).astype(BF16)).astype(BF16)
-    taps = [jnp.concatenate([cmid_ref[dy, dx].astype(F32) for dx in range(3)], axis=0) for dy in range(3)]
+        band_ref[w] = dot(taps_t, jnp.where(pick, 0.5, 0.0).astype(BF16)).astype(BF16)
+    taps = [0.5 * jnp.concatenate([cmid_ref[dy, dx].astype(F32) for dx in range(3)], axis=0) for dy in range(3)]
     outer = 0.5 * (taps[0] + taps[2])
     for v, mid in enumerate((taps[0], outer + 0.5 * taps[1], outer - 0.5 * taps[1], taps[2])):
         mid_ref[v] = mid.astype(BF16).T
-    weight = tw_ref[...].T
+    weight = 0.5 * tw_ref[...].T
     high = weight.astype(BF16)
     low = (weight - high.astype(F32)).astype(BF16)
     twt_ref[...] = jnp.concatenate([high, high, low], axis=1)
     qkvt_ref[...] = qkv_ref[...].T
-    wot_ref[...] = wo_ref[...].T
+    wot_ref[...] = (0.5 * wo_ref[...].astype(F32)).astype(BF16).T
     wet_ref[...] = jnp.concatenate([we_ref[...].astype(F32), jnp.zeros((12, CH), F32)], axis=0).astype(BF16)
     gain_out[...] = jnp.broadcast_to(gain_ref[...].reshape(1, CH), (FR, CH)).T
-    key_slot = lax.broadcasted_iota(jnp.int32, (FR, FR), 0)
-    query_slot = lanes((FR, FR))
-    near_ref[...] = jnp.where(jnp.abs(key_slot - query_slot) <= WIN, 1.0, 0.0).astype(BF16)
+    key_slot = lax.broadcasted_iota(jnp.int32, (FR, 2 * FR), 0)
+    query_slot = lanes((FR, 2 * FR)) & (FR - 1)
+    near_ref[...] = jnp.where(jnp.abs(key_slot - query_slot) <= WIN, 1.0, 0.0)
     lane = lanes((8, FR))
     for s in range(STEPS):
         rows = jnp.concatenate([ent_ref[s, c, r : r + 1, :] for c in range(4) for r in range(2)], axis=0)
@@ -143,14 +142,11 @@
             ent_out[s, 8 * i : 8 * i + 8, :] = jnp.where(lane == FR - 1, shifted, 0.0)
 
 
-def blank(query_ref, value_ref, weight_ref):
+def blank(query_ref):
     def body(i, carry):
         for p in range(5):
             query_ref[i, p, :HD, FR:] = jnp.zeros((HD, FR), BF16)
             query_ref[i, p, HD:, :FR] = jnp.zeros((HD, FR), BF16)
-            value_ref[i, p, HD:] = jnp.ones((16, 2 * FR), BF16)
-            weight_ref[i, p, :FR, FR:] = jnp.zeros((FR, FR), BF16)
-            weight_ref[i, p, FR:, :FR] = jnp.zeros((FR, FR), BF16)
         return carry
 
     lax.fori_loop(0, PX, body, 0)
@@ -197,9 +193,9 @@
                 hidden = both[:, half * FR : (half + 1) * FR] + emb_ref[...]
                 if p != half:
                     hid_ref[w, p] = hidden
-                    active.append(jnp.where(inside, silu(hidden), 0.0))
+                    active.append(jnp.where(inside, silu_of_half(hidden), 0.0))
                 else:
-                    active.append(jnp.where(inside & ((t > 0) if p == 0 else (t < NT - 1)), silu(hidden), 0.0))
+                    active.append(jnp.where(inside & ((t > 0) if p == 0 else (t < NT - 1)), silu_of_half(hidden), 0.0))
         a0, a1, a2, a3 = active
         for v, part in enumerate((a0 - a2, a1 + a2, a2 - a1, a1 - a3)):
             act_ref[w, v] = part.astype(BF16)
@@ -227,14 +223,14 @@
 
 
 def block_net(hs_ref, mid_ref, qkvt_ref, wot_ref, wet_ref, gain_ref, near_ref, hid_ref, act_ref, noise_ref,
-              block_ref, normed_ref, project_ref, query_ref, stack_ref, key_ref, value_ref, weight_ref, mixed_ref):
+              block_ref, normed_ref, project_ref, query_ref, stack_ref, key_ref, value_ref, weight_ref, total_ref, mixed_ref):
     def norm(i, block):
         block_ref[i] = block
         center = jnp.mean(block, axis=0, keepdims=True)
         moved = block - center
         spread = jnp.mean(moved * moved, axis=0, keepdims=True)
         gain = jnp.concatenate([gain_ref[...]] * 2, axis=1)
-        normed_ref[i] = (moved * lax.rsqrt(spread + 1e-05) * gain).astype(BF16)
+        normed_ref[i] = (moved * lax.rsqrt(spread + 1e-05 / 4) * gain).astype(BF16)
 
     def conv_mid(j):
         parts = []
@@ -255,29 +251,25 @@
                 part = lambda k: project_ref[i, k * CH + h * HD : k * CH + (h + 1) * HD, cut]
                 query_ref[i, p, n * HD : (n + 1) * HD, own] = unit(part(0), hs_ref[h] * math.log2(math.e))
                 stack_ref[i, p, n * HD : (n + 1) * HD] = unit(part(1), 1.0)
-                value_ref[i, p, :HD, own] = part(2).astype(BF16)
+                value_ref[i, p, :, own] = part(2).astype(BF16)
             key_ref[i, p] = stack_ref[i, p].T
 
     def attend(i):
         for p in range(5):
-            weights = jnp.exp2(dot(key_ref[i, p], query_ref[i, p])).astype(BF16)
-            for n in range(2):
-                own = slice(n * FR, (n + 1) * FR)
-                weight_ref[i, p, own, own] = weights[:, own] * near_ref[...]
+            weights = jnp.exp2(dot(key_ref[i, p], query_ref[i, p])) * near_ref[...]
+            total_ref[i, p] = jnp.sum(weights, axis=0, keepdims=True)
+            weight_ref[i, p] = weights.astype(BF16)
 
     def mix(i):
-        for p, ((s, h), _) in enumerate(places()):
-            total = dot(value_ref[i, p], weight_ref[i, p])
-            part = (total[:HD] * (1.0 / total[HD : HD + 1])).astype(BF16)
-            if p == 4:
-                mixed_ref[i, h * HD :, :] = part
-            else:
-                cut = slice(s * FR, (s + 1) * FR)
-                mixed_ref[i, h * HD : (h + 1) * HD, cut] = part[:, :FR]
-                mixed_ref[i, (h + 1) * HD : (h + 2) * HD, cut] = part[:, FR:]
+        for p, pair in enumerate(places()):
+            share = 1.0 / total_ref[i, p]
+            for n, (s, h) in enumerate(pair):
+                cut, own = slice(s * FR, (s + 1) * FR), slice(n * FR, (n + 1) * FR)
+                part = dot(value_ref[i, p, :, own], weight_ref[i, p, :, own]) * share[:, own]
+                mixed_ref[i, h * HD : (h + 1) * HD, cut] = part.astype(BF16)
 
     def upper(i):
-        normed_ref[i] = silu(block_ref[i] + dot(wot_ref[...], mixed_ref[i])).astype(BF16)
+        normed_ref[i] = silu_of_half(block_ref[i] + dot(wot_ref[...], mixed_ref[i])).astype(BF16)
 
     def noise(i):
         noise_ref[i] = dot(wet_ref[...], normed_ref[i])[:8]
@@ -313,7 +305,7 @@
            lat_ref, ent_ref, lev_ref, tw_ref, cin_ref, cmid_ref, gain_ref, qkv_ref, hs_ref, wo_ref, we_ref, taps_ref,
            twt_ref, band_ref, mid_ref, qkvt_ref, wot_ref, wet_ref, gain_out, near_ref, ent_out,
            emb_ref, rhs_ref, hid_ref, act_ref, noise_ref,
-           block_ref, normed_ref, project_ref, query_ref, stack_ref, key_ref, value_ref, weight_ref, mixed_ref,
+           block_ref, normed_ref, project_ref, query_ref, stack_ref, key_ref, value_ref, weight_ref, total_ref, mixed_ref,
            send1, recv1, halo, state_ref, own_ref, left_ref, right_ref, send3, recv3,
            load_sem, send1_sem, recv1_sem, send2_sem, recv2_sem, send3_sem, recv3_sem):
     q, t = lax.axis_index("queue"), lax.axis_index("tile")
@@ -364,7 +356,7 @@
         load.wait()
     prepare(cin_ref, cmid_ref, gain_ref, qkv_ref, wo_ref, we_ref, ent_ref, tw_ref, taps_ref,
             twt_ref, band_ref, mid_ref, qkvt_ref, wot_ref, wet_ref, gain_out, near_ref, ent_out, g)
-    blank(query_ref, value_ref, weight_ref)
+    blank(query_ref)
 
     def settle(ref, sem, count):
         part = ref.at[pl.ds(0, count)]
@@ -384,7 +376,7 @@
 
     conv_in(slots, band_ref, emb_ref, rhs_ref, hid_ref, act_ref, g, t)
     block_net(hs_ref, mid_ref, qkvt_ref, wot_ref, wet_ref, gain_out, near_ref, hid_ref, act_ref, noise_ref,
-              block_ref, normed_ref, project_ref, query_ref, stack_ref, key_ref, value_ref, weight_ref, mixed_ref)
+              block_ref, normed_ref, project_ref, query_ref, stack_ref, key_ref, value_ref, weight_ref, total_ref, mixed_ref)
     state = advance(state, noise_ref, alpha, beta, ent_out[0])
 
     state_ref[...] = state
@@ -420,7 +412,7 @@
 
     conv_in(slots, band_ref, emb_ref, rhs_ref, hid_ref, act_ref, g, t)
     block_net(hs_ref, mid_ref, qkvt_ref, wot_ref, wet_ref, gain_out, near_ref, hid_ref, act_ref, noise_ref,
-              block_ref, normed_ref, project_ref, query_ref, stack_ref, key_ref, value_ref, weight_ref, mixed_ref)
+              block_ref, normed_ref, project_ref, query_ref, stack_ref, key_ref, value_ref, weight_ref, total_ref, mixed_ref)
     state = advance(state_ref[...], noise_ref, alpha, beta, ent_out[1])
 
     frames = jnp.concatenate([state, jnp.zeros((64, FR), F32)], axis=0).T
@@ -472,12 +464,13 @@
             v((40, CH), F32),
             v((CH, 3 * CH), BF16),
             v((PX + 2, CH, TAPS), BF16), v((4, CH, 3 * CH), BF16), v((3 * CH, CH), BF16), v((CH, CH), BF16),
-            v((16, CH), BF16), v((CH, FR), F32), v((FR, FR), BF16), v((STEPS, 64, FR), F32),
+            v((16, CH), BF16), v((CH, FR), F32), v((FR, 2 * FR), F32), v((STEPS, 64, FR), F32),
             v((CH, FR), F32), v((2, TAPS, 2 * FR), BF16), v((PX + 2, 2, CH, FR), F32),
             v((PX + 2, 4, CH, FR), BF16), v((PX, 8, 2 * FR), F32),
             v((PX, CH, 2 * FR), F32), v((PX, CH, 2 * FR), BF16), v((PX, 3 * CH, 2 * FR), F32),
             v((PX, 5, FR, 2 * FR), BF16), v((PX, 5, FR, FR), BF16), v((PX, 5, FR, FR), BF16),
-            v((PX, 5, HD + 16, 2 * FR), BF16), v((PX, 5, 2 * FR, 2 * FR), BF16), v((PX, CH, 2 * FR), BF16),
+            v((PX, 5, HD, 2 * FR), BF16), v((PX, 5, FR, 2 * FR), BF16), v((PX, 5, 1, 2 * FR), F32),
+            v((PX, CH, 2 * FR), BF16),
             v((NQ, 8, FR), F32), v((3, FR, FR), F32), v((3, 2 * ROW, FR), BF16), v((64, FR), F32), v((64, FR), BF16),
             v((16, FR), BF16), v((16, FR), BF16), v((NQ, 8, FR), F32), v((NQ, 8, FR), F32),
             dma((len(inputs),)), dma((3,)), dma((3,)), dma((8,)), dma((8,)), dma((1,)), dma((1,)),

time: 44 us -> 42.5 us (0.966)
  Pallas kernels: 43.3 us -> 41.8 us
    pallas_call x1, Pallas kernels: 43.3 us -> 41.8 us  [per_device(): pl.pallas_call(kernel, out_shape=pltpu.VMEM(queue_latents.shape, F32), in...]
where the time goes in v5:
time: 42.5 us; the launch traced here: 42.4 us
  Pallas kernels  41.8 us (98%)
  local copies, waits for them, and re-layouts  0.62 us (1%)
    pallas_call x1, Pallas kernels, per_device(): pl.pallas_call(kernel, out_shape=pltpu.VMEM(queue_latents.shape, F32), in...  41.8 us

profile of v5, /device:TPU:1, one launch (start us, length us, event | category | flops | bytes accessed | tf_op | source)
XLA Modules:
  0.0 42.4 jit_solution(10231385516969258846)
XLA Ops:
  0.0 41.8 %shard_map.109 = f32[8,4,2,128]{3,2,1,0:T(2,128)S(1)} custom-call(f32[8,4,2,128]{3,2,1,0:T(2,128)} %lat_hbm.1, f32[2,4,2,128]{3,2,1,0:T(2,128)} %ent_hbm.1, s32[8]{0:T(128)} %lev_hbm.1, f32[320,320]{1,0:T(8,128)} %tw_hbm.1, bf16[3,3,4,320]{3,2,1,0:T(4,128)(2,1)} %cin_hbm.1, bf16[3,3,320,320]{3,2,1,0:T(8,128)(2,1)} %cmid_hbm.1, f32[320]{0:T(512)} %gain_hbm.1, ...), custom_call_target="tpu_custom_call" | custom-call | tf_op jit(solution)/shard_map/pallas_call | solution.py:457
  41.8 0.6 %copy.13 = f32[8,4,2,128]{3,2,1,0:T(2,128)} copy(f32[8,4,2,128]{3,2,1,0:T(2,128)S(1)} %shard_map.109) | data formatting | bytes 65536

commit v6 on v5

--- a/solution.py
+++ b/solution.py
@@ -100,7 +100,7 @@
 
 
 def prepare(cin_ref, cmid_ref, gain_ref, qkv_ref, wo_ref, we_ref, ent_ref, tw_ref, taps_ref,
-            twt_ref, band_ref, mid_ref, qkvt_ref, wot_ref, wet_ref, gain_out, near_ref, ent_out, g):
+            twt_ref, band_ref, mid_ref, qkvt_ref, wot_ref, wet_ref, near_ref, ent_out, g):
     taps_ref[...] = jnp.zeros(taps_ref.shape, F32)
     for i in range(9):
         taps_ref[4 * i : 4 * i + 4, :] = cin_ref[i // 3, i % 3].astype(F32)
@@ -125,10 +125,9 @@
     high = weight.astype(BF16)
     low = (weight - high.astype(F32)).astype(BF16)
     twt_ref[...] = jnp.concatenate([high, high, low], axis=1)
-    qkvt_ref[...] = qkv_ref[...].T
+    qkvt_ref[...] = (qkv_ref[...].T.astype(F32) * gain_ref[...].reshape(1, CH)).astype(BF16)
     wot_ref[...] = (0.5 * wo_ref[...].astype(F32)).astype(BF16).T
     wet_ref[...] = jnp.concatenate([we_ref[...].astype(F32), jnp.zeros((12, CH), F32)], axis=0).astype(BF16)
-    gain_out[...] = jnp.broadcast_to(gain_ref[...].reshape(1, CH), (FR, CH)).T
     key_slot = lax.broadcasted_iota(jnp.int32, (FR, 2 * FR), 0)
     query_slot = lanes((FR, 2 * FR)) & (FR - 1)
     near_ref[...] = jnp.where(jnp.abs(key_slot - query_slot) <= WIN, 1.0, 0.0)
@@ -152,14 +151,17 @@
     lax.fori_loop(0, PX, body, 0)
 
 
-def embed(level, twt_ref, emb_ref):
+def embed(level, twt_ref, emb_ref, t):
     index = lax.broadcasted_iota(jnp.int32, (CH // 2, FR), 0).astype(F32)
     freqs = jnp.exp(-math.log(10000.0) * index / (CH // 2))
     sine, cosine = sin_cos(level * freqs)
     feature = jnp.concatenate([sine, cosine], axis=0)
     high = feature.astype(BF16)
     low = (feature - high.astype(F32)).astype(BF16)
-    emb_ref[...] = dot(twt_ref[...], jnp.concatenate([high, low, high], axis=0))
+    emb = dot(twt_ref[...], jnp.concatenate([high, low, high], axis=0))
+    emb_ref[0] = jnp.where(t > 0, emb, 0.0)
+    emb_ref[1] = emb
+    emb_ref[2] = jnp.where(t < NT - 1, emb, 0.0)
 
 
 def coefficients(level):
@@ -181,27 +183,28 @@
                 [slot[k * 16 + r * 8 : k * 16 + r * 8 + 8] for k in range(6)], axis=0).astype(BF16))
     for p in range(2):
         for half in range(2):
-            rhs_ref[p, :, half * FR : (half + 1) * FR] = jnp.concatenate(
-                rows[2 * p + half : 2 * p + half + 3], axis=0)
-
-    def body(w, carry):
-        inside = ((w > 0) | (g > 0)) & ((w < PX + 1) | (g < NQ - 1))
+            near = jnp.concatenate(rows[2 * p + half : 2 * p + half + 3], axis=0)
+            if p == half:
+                near = jnp.where((t > 0) if p == 0 else (t < NT - 1), near, jnp.zeros_like(near))
+            rhs_ref[p, :, half * FR : (half + 1) * FR] = near
+
+    def column(w, inside=None):
         active = []
         for p in range(2):
             both = dot(band_ref[w], rhs_ref[p])
             for half in range(2):
-                hidden = both[:, half * FR : (half + 1) * FR] + emb_ref[...]
+                hidden = both[:, half * FR : (half + 1) * FR] + emb_ref[p + half]
                 if p != half:
                     hid_ref[w, p] = hidden
-                    active.append(jnp.where(inside, silu_of_half(hidden), 0.0))
-                else:
-                    active.append(jnp.where(inside & ((t > 0) if p == 0 else (t < NT - 1)), silu_of_half(hidden), 0.0))
+                hidden = silu_of_half(hidden)
+                active.append(hidden if inside is None else jnp.where(inside, hidden, 0.0))
         a0, a1, a2, a3 = active
         for v, part in enumerate((a0 - a2, a1 + a2, a2 - a1, a1 - a3)):
             act_ref[w, v] = part.astype(BF16)
-        return carry
-
-    lax.fori_loop(0, PX + 2, body, 0, unroll=PX + 2)
+
+    column(0, g > 0)
+    lax.fori_loop(1, PX + 1, lambda w, carry: (column(w), carry)[1], 0, unroll=PX)
+    column(PX + 1, g < NQ - 1)
 
 
 def unit(x, scale):
@@ -222,15 +225,14 @@
     return pairs + [((0, 4), (1, 4))]
 
 
-def block_net(hs_ref, mid_ref, qkvt_ref, wot_ref, wet_ref, gain_ref, near_ref, hid_ref, act_ref, noise_ref,
+def block_net(hs_ref, mid_ref, qkvt_ref, wot_ref, wet_ref, near_ref, hid_ref, act_ref, noise_ref,
               block_ref, normed_ref, project_ref, query_ref, stack_ref, key_ref, value_ref, weight_ref, total_ref, mixed_ref):
     def norm(i, block):
         block_ref[i] = block
         center = jnp.mean(block, axis=0, keepdims=True)
         moved = block - center
         spread = jnp.mean(moved * moved, axis=0, keepdims=True)
-        gain = jnp.concatenate([gain_ref[...]] * 2, axis=1)
-        normed_ref[i] = (moved * lax.rsqrt(spread + 1e-05 / 4) * gain).astype(BF16)
+        normed_ref[i] = (moved * lax.rsqrt(spread + 1e-05 / 4)).astype(BF16)
 
     def conv_mid(j):
         parts = []
@@ -303,7 +305,7 @@
 def kernel(lat_hbm, ent_hbm, lev_hbm, tw_hbm, cin_hbm, cmid_hbm, gain_hbm, qkv_hbm, hs_hbm, wo_hbm, we_hbm,
            out_ref,
            lat_ref, ent_ref, lev_ref, tw_ref, cin_ref, cmid_ref, gain_ref, qkv_ref, hs_ref, wo_ref, we_ref, taps_ref,
-           twt_ref, band_ref, mid_ref, qkvt_ref, wot_ref, wet_ref, gain_out, near_ref, ent_out,
+           twt_ref, band_ref, mid_ref, qkvt_ref, wot_ref, wet_ref, near_ref, ent_out,
            emb_ref, rhs_ref, hid_ref, act_ref, noise_ref,
            block_ref, normed_ref, project_ref, query_ref, stack_ref, key_ref, value_ref, weight_ref, total_ref, mixed_ref,
            send1, recv1, halo, state_ref, own_ref, left_ref, right_ref, send3, recv3,
@@ -355,7 +357,7 @@
     for load in loads[2:]:
         load.wait()
     prepare(cin_ref, cmid_ref, gain_ref, qkv_ref, wo_ref, we_ref, ent_ref, tw_ref, taps_ref,
-            twt_ref, band_ref, mid_ref, qkvt_ref, wot_ref, wet_ref, gain_out, near_ref, ent_out, g)
+            twt_ref, band_ref, mid_ref, qkvt_ref, wot_ref, wet_ref, near_ref, ent_out, g)
     blank(query_ref)
 
     def settle(ref, sem, count):
@@ -369,13 +371,13 @@
             settle(recv1.at[slot], recv1_sem.at[slot], FR)
     slots = [recv1[slot].T for slot in range(3)]
     level = slots[1][2 * ROW : 2 * ROW + 1]
-    embed(level, twt_ref, emb_ref)
+    embed(level, twt_ref, emb_ref, t)
     alpha, beta = coefficients(level)
     state = slots[1][:64]
     slots = [masked(slot[: 2 * ROW], i, g, t) for i, slot in enumerate(slots)]
 
     conv_in(slots, band_ref, emb_ref, rhs_ref, hid_ref, act_ref, g, t)
-    block_net(hs_ref, mid_ref, qkvt_ref, wot_ref, wet_ref, gain_out, near_ref, hid_ref, act_ref, noise_ref,
+    block_net(hs_ref, mid_ref, qkvt_ref, wot_ref, wet_ref, near_ref, hid_ref, act_ref, noise_ref,
               block_ref, normed_ref, project_ref, query_ref, stack_ref, key_ref, value_ref, weight_ref, total_ref, mixed_ref)
     state = advance(state, noise_ref, alpha, beta, ent_out[0])
 
@@ -411,7 +413,7 @@
     slots = [masked(halo[i].astype(F32), i, g, t) for i in range(3)]
 
     conv_in(slots, band_ref, emb_ref, rhs_ref, hid_ref, act_ref, g, t)
-    block_net(hs_ref, mid_ref, qkvt_ref, wot_ref, wet_ref, gain_out, near_ref, hid_ref, act_ref, noise_ref,
+    block_net(hs_ref, mid_ref, qkvt_ref, wot_ref, wet_ref, near_ref, hid_ref, act_ref, noise_ref,
               block_ref, normed_ref, project_ref, query_ref, stack_ref, key_ref, value_ref, weight_ref, total_ref, mixed_ref)
     state = advance(state_ref[...], noise_ref, alpha, beta, ent_out[1])
 
@@ -464,8 +466,8 @@
             v((40, CH), F32),
             v((CH, 3 * CH), BF16),
             v((PX + 2, CH, TAPS), BF16), v((4, CH, 3 * CH), BF16), v((3 * CH, CH), BF16), v((CH, CH), BF16),
-            v((16, CH), BF16), v((CH, FR), F32), v((FR, 2 * FR), F32), v((STEPS, 64, FR), F32),
-            v((CH, FR), F32), v((2, TAPS, 2 * FR), BF16), v((PX + 2, 2, CH, FR), F32),
+            v((16, CH), BF16), v((FR, 2 * FR), F32), v((STEPS, 64, FR), F32),
+            v((3, CH, FR), F32), v((2, TAPS, 2 * FR), BF16), v((PX + 2, 2, CH, FR), F32),
             v((PX + 2, 4, CH, FR), BF16), v((PX, 8, 2 * FR), F32),
             v((PX, CH, 2 * FR), F32), v((PX, CH, 2 * FR), BF16), v((PX, 3 * CH, 2 * FR), F32),
             v((PX, 5, FR, 2 * FR), BF16), v((PX, 5, FR, FR), BF16), v((PX, 5, FR, FR), BF16),

time: 42.5 us -> 42.3 us (level)
  no operation moved by 1% of the time
where the time goes in v6:
time: 42.3 us; the launch traced here: 42.2 us
  Pallas kernels  41.6 us (98%)
  local copies, waits for them, and re-layouts  0.62 us (1%)
    pallas_call x1, Pallas kernels, per_device(): pl.pallas_call(kernel, out_shape=pltpu.VMEM(queue_latents.shape, F32), in...  41.6 us

profile of v6, /device:TPU:1, one launch (start us, length us, event | category | flops | bytes accessed | tf_op | source)
XLA Modules:
  0.0 42.2 jit_solution(3640016361361797849)
XLA Ops:
  0.0 41.6 %shard_map.109 = f32[8,4,2,128]{3,2,1,0:T(2,128)S(1)} custom-call(f32[8,4,2,128]{3,2,1,0:T(2,128)} %lat_hbm.1, f32[2,4,2,128]{3,2,1,0:T(2,128)} %ent_hbm.1, s32[8]{0:T(128)} %lev_hbm.1, f32[320,320]{1,0:T(8,128)} %tw_hbm.1, bf16[3,3,4,320]{3,2,1,0:T(4,128)(2,1)} %cin_hbm.1, bf16[3,3,320,320]{3,2,1,0:T(8,128)(2,1)} %cmid_hbm.1, f32[320]{0:T(512)} %gain_hbm.1, ...), custom_call_target="tpu_custom_call" | custom-call | tf_op jit(solution)/shard_map/pallas_call | solution.py:459
  41.6 0.6 %copy.13 = f32[8,4,2,128]{3,2,1,0:T(2,128)} copy(f32[8,4,2,128]{3,2,1,0:T(2,128)S(1)} %shard_map.109) | data formatting | bytes 65536

commit v7 on v6

--- a/solution.py
+++ b/solution.py
@@ -401,14 +401,14 @@
             sent_too, got_too = (t > 0, t < NT - 1) if down == -1 else (t < NT - 1, t > 0) if down == 1 else (None, None)
             both_of = lambda a, b: b if a is None else a if b is None else a & b
             i = len(copies)
-            copies.append((both_of(sent, sent_too), both_of(got, got_too), pltpu.make_async_remote_copy(
-                src_ref=src, dst_ref=halo.at[1 - down, pl.ds(start, size)],
-                send_sem=send2_sem.at[i], recv_sem=recv2_sem.at[i],
-                device_id=(peer, t + down), device_id_type=MESH)))
-    for sent, _, copy in copies:
+            part = halo.at[1 - down, pl.ds(start, size)]
+            copies.append((both_of(sent, sent_too), both_of(got, got_too), part, pltpu.make_async_remote_copy(
+                src_ref=src, dst_ref=part, send_sem=send2_sem.at[i], recv_sem=recv2_sem.at[i],
+                device_id=(peer, jnp.clip(t + down, 0, NT - 1)), device_id_type=MESH)))
+    for sent, _, _, copy in copies:
         pl.when(sent)(copy.start)
-    for _, got, copy in copies:
-        pl.when(got)(copy.wait_recv)
+    for i, (_, got, part, _) in enumerate(copies):
+        pl.when(got)(lambda: pltpu.make_async_copy(part, part, recv2_sem.at[i]).wait())
     halo[1, :64] = own_ref[...]
     slots = [masked(halo[i].astype(F32), i, g, t) for i in range(3)]
 
@@ -427,7 +427,7 @@
             send_sem=send3_sem.at[0], recv_sem=recv3_sem.at[0],
             device_id=(peer, t), device_id_type=MESH).start()
     recv3[g] = send3[q]
-    for sent, _, copy in copies:
+    for sent, _, _, copy in copies:
         pl.when(sent)(copy.wait_send)
     settle(send1, send1_sem.at[1], NQ - 1)
     for there, _, slot in sides:

time: 42.3 us -> 42.3 us (level)
  no operation moved by 1% of the time
where the time goes in v7:
time: 42.3 us; the launch traced here: 42.2 us
  Pallas kernels  41.6 us (98%)
  local copies, waits for them, and re-layouts  0.62 us (1%)
    pallas_call x1, Pallas kernels, per_device(): pl.pallas_call(kernel, out_shape=pltpu.VMEM(queue_latents.shape, F32), in...  41.6 us

profile of v7, /device:TPU:1, one launch (start us, length us, event | category | flops | bytes accessed | tf_op | source)
XLA Modules:
  0.0 42.2 jit_solution(10041836193558260399)
XLA Ops:
  0.0 41.6 %shard_map.109 = f32[8,4,2,128]{3,2,1,0:T(2,128)S(1)} custom-call(f32[8,4,2,128]{3,2,1,0:T(2,128)} %lat_hbm.1, f32[2,4,2,128]{3,2,1,0:T(2,128)} %ent_hbm.1, s32[8]{0:T(128)} %lev_hbm.1, f32[320,320]{1,0:T(8,128)} %tw_hbm.1, bf16[3,3,4,320]{3,2,1,0:T(4,128)(2,1)} %cin_hbm.1, bf16[3,3,320,320]{3,2,1,0:T(8,128)(2,1)} %cmid_hbm.1, f32[320]{0:T(512)} %gain_hbm.1, ...), custom_call_target="tpu_custom_call" | custom-call | tf_op jit(solution)/shard_map/pallas_call | solution.py:459
  41.6 0.6 %copy.13 = f32[8,4,2,128]{3,2,1,0:T(2,128)} copy(f32[8,4,2,128]{3,2,1,0:T(2,128)S(1)} %shard_map.109) | data formatting | bytes 65536
